TPU v7x, 32 devices: a whole 2x2x4 slice. The times are simulated.
32 devices in a mesh: frame: 16 (over z, x, core), band: 2 (over y).
Axes of the slice: x: 2, y: 2, z: 4, core: 2. Of those that a mesh axis runs over, the one named last changes fastest.
Arguments:
- frames: bfloat16 [128, 16, 16, 320], P('frame', 'band'), may hold values from -6 to 6
- control: bfloat16 [128, 16, 16, 320], P('frame', 'band'), may hold values from -4 to 4
- conv_first: bfloat16 [3, 3, 320, 320], replicated, may hold values from -0.109375 to 0.109375
- conv_second: bfloat16 [3, 3, 320, 320], replicated, may hold values from -0.109375 to 0.109375
- time_table: float32 [1000, 320], replicated, may hold values from -5 to 5
- step_index: int32 [1], replicated, may hold values from 0 to 999
- norm_gain: float32 [320], replicated, may hold values from 0.5 to 1.5
- w_query: bfloat16 [320, 320], replicated, as said below
- w_key: bfloat16 [320, 320], replicated, as said below
- w_value: bfloat16 [320, 320], replicated, may hold values from -0.3125 to 0.3125
- w_out: bfloat16 [320, 320], replicated, may hold values from -0.3125 to 0.3125
- rel_bias: float32 [8, 33], replicated, may hold values from -4 to 4
- reach: int32 [128], replicated, may hold values from 4 to 16, as said below
Outputs:
- section_out: float32 [128, 16, 16, 320], P('frame', 'band')
Inputs may be any that keep to these rules, and one draw needn't show every extreme that they name: Each frame attends within reach[f] frames on the loop; the first and last frame of each aligned block of 8 frames have reach 16. `w_query`: projection into 8 heads. `w_key`: projection into 8 heads.
All inputs are finite; a program needn't handle non-finite values.
Results may differ from a plain program's by a relative error of at most 0.012.
The roundings to bfloat16 on the way count: a program that leaves them out, or rounds other values in their place, can miss the bound.
Values may be sent and summed in bfloat16 or wider, within the bound.
A program may use at most 128 MiB of HBM per device.

v0:
```python
import jax
import jax.numpy as jnp
from jax import lax
from jax.sharding import PartitionSpec as P


def with_halo(block, sides, width):
    for axis, dim in sides:
        count = lax.axis_size(axis)
        forward = [(i, i + 1) for i in range(count - 1)]
        backward = [(target, source) for source, target in forward]
        low = lax.ppermute(
            lax.slice_in_dim(block, block.shape[dim] - width, None, axis=dim), axis, forward
        )
        high = lax.ppermute(lax.slice_in_dim(block, 0, width, axis=dim), axis, backward)
        block = jnp.concatenate([low, block, high], axis=dim)
    return block


def passed_along(block, axis, distance):
    devices = range(lax.axis_size(axis))
    route = [((i - distance) % len(devices), i) for i in devices]
    return lax.ppermute(block, axis, route)


def conv_pass(field, weight):
    rimmed = with_halo(field, (("band", 1),), 1)
    return lax.conv_general_dilated(
        rimmed,
        weight,
        (1, 1),
        ((0, 0), (1, 1)),
        dimension_numbers=("NHWC", "HWIO", "NHWC"),
        preferred_element_type=jnp.float32,
    )


def attend(query, key, value, q_frames, k_frames, reach_q, rel_bias, total):
    heads = rel_bias.shape[0]
    span = (rel_bias.shape[1] - 1) // 2
    fq, pix, chans = query.shape
    fk = key.shape[0]
    dh = chans // heads
    q4 = query.reshape(fq, pix, heads, dh)
    k4 = key.reshape(fk, pix, heads, dh)
    v4 = value.reshape(fk, pix, heads, dh)
    scores = jnp.einsum("iphd,jphd->phij", q4, k4, preferred_element_type=jnp.float32) * dh ** (
        -0.5
    )
    delta = (k_frames[None, :] - q_frames[:, None] + total // 2) % total - total // 2
    table = (
        delta[:, :, None] + span == jnp.arange(2 * span + 1, dtype=jnp.int32)[None, None, :]
    ).astype(jnp.float32)
    bias = jnp.einsum("ijs,hs->hij", table, rel_bias, precision=lax.Precision.HIGHEST)
    allowed = jnp.abs(delta) <= reach_q[:, None]
    scores = jnp.where(allowed[None, None], scores + bias[None], -jnp.inf)
    top = jnp.max(scores, axis=-1, keepdims=True)
    expo = jnp.exp(scores - top)
    weights = (expo / jnp.sum(expo, axis=-1, keepdims=True)).astype(jnp.bfloat16)
    out = jnp.einsum("phij,jphd->iphd", weights, v4, preferred_element_type=jnp.float32)
    return out.astype(jnp.bfloat16).reshape(fq, pix, chans)


def shards(
    frames,
    control,
    conv_first,
    conv_second,
    time_table,
    step_index,
    norm_gain,
    w_query,
    w_key,
    w_value,
    w_out,
    rel_bias,
    reach,
):
    count, rows, cols, chans = frames.shape
    pixels = rows * cols
    members = lax.axis_size("frame")
    total = count * members
    start = lax.axis_index("frame") * count
    picker = (jnp.arange(time_table.shape[0], dtype=jnp.int32) == step_index[0]).astype(jnp.float32)
    embed = jnp.dot(picker, time_table, precision=lax.Precision.HIGHEST)
    merged = (frames.astype(jnp.float32) + control.astype(jnp.float32)).astype(jnp.bfloat16)
    activated = jax.nn.silu(conv_pass(merged, conv_first) + embed).astype(jnp.bfloat16)
    block_out = merged.astype(jnp.float32) + conv_pass(activated, conv_second)
    flat = block_out.reshape(count * pixels, chans)
    centre = flat - jnp.mean(flat, axis=1, keepdims=True)
    normed = (
        centre * lax.rsqrt(jnp.mean(centre * centre, axis=1, keepdims=True) + 1e-05) * norm_gain
    ).astype(jnp.bfloat16)
    query = (
        jnp.dot(normed, w_query, preferred_element_type=jnp.float32)
        .astype(jnp.bfloat16)
        .reshape(count, pixels, chans)
    )
    key = (
        jnp.dot(normed, w_key, preferred_element_type=jnp.float32)
        .astype(jnp.bfloat16)
        .reshape(count, pixels, chans)
    )
    value = (
        jnp.dot(normed, w_value, preferred_element_type=jnp.float32)
        .astype(jnp.bfloat16)
        .reshape(count, pixels, chans)
    )
    span = (rel_bias.shape[1] - 1) // 2
    hops = -(-span // count)
    stacked = jnp.stack((key, value))
    pieces = []
    key_frames = []
    for offset in list(range(hops, 0, -1)) + [0] + list(range(-1, -hops - 1, -1)):
        if offset == 0:
            pieces.append(stacked)
        else:
            pieces.append(passed_along(stacked, "frame", offset))
        key_frames.append((start - offset * count + jnp.arange(count, dtype=jnp.int32)) % total)
    window = jnp.concatenate(pieces, axis=1)
    q_frames = start + jnp.arange(count, dtype=jnp.int32)
    reach_q = lax.dynamic_slice_in_dim(reach, start, count)
    attended = attend(
        query, window[0], window[1], q_frames, jnp.concatenate(key_frames), reach_q, rel_bias, total
    )
    mixed = jnp.dot(
        attended.reshape(count * pixels, chans), w_out, preferred_element_type=jnp.float32
    )
    return (flat + mixed).reshape(count, rows, cols, chans)


def solution(mesh):
    in_specs = (
        P("frame", "band", None, None),
        P("frame", "band", None, None),
        P(),
        P(),
        P(),
        P(),
        P(),
        P(),
        P(),
        P(),
        P(),
        P(),
        P(),
    )
    out_specs = P("frame", "band", None, None)
    return jax.shard_map(shards, mesh=mesh, in_specs=in_specs, out_specs=out_specs, check_vma=False)
```

profile of v0, /device:TPU:1, one launch (start us, length us, event | category | flops | bytes accessed | tf_op | source)
XLA Modules:
  0.0 187.7 jit_solution(4901209764603564483)
XLA Ops:
  0.0 2.4 %add_convert_fusion = bf16[8,8,16,320]{3,0,2,1:T(8,128)(2,1)S(1)} fusion(bf16[8,8,16,320]{3,2,1,0:T(8,128)(2,1)} %param.14, bf16[8,8,16,320]{3,2,1,0:T(8,128)(2,1)} %param.13), kind=kLoop, calls=%fused_computation.16 | loop fusion | flops 1310720 | bytes 1966080 | tf_op jit(solution)/shard_map/convert_element_type | solution.py:86
  2.4 4.0 %collective-permute-start = (bf16[8,1,16,320]{3,0,2,1:T(8,128)(2,1)S(1)}, bf16[8,1,16,320]{3,0,2,1:T(8,128)(2,1)S(1)}, u32[]{:S(2)}, u32[]{:S(2)}) collective-permute-start(bf16[8,1,16,320]{3,0,2,1:T(8,128)(2,1)S(1)} %get-tuple-element.9), channel_id=1, source_target_pairs={{0,1},{2,3},{4,5},{6,7},{8,9},{10,11},{12,13},{14,15},{16,17},{18,... | collective-permute-start | bytes 245768 | tf_op jit(solution)/shard_map/ppermute | solution.py:12
  6.4 1.3 collective-permute-start.1
  8.4 0.7 convolution_reduce_fusion
  9.1 2.7 %collective-permute-done.1 = bf16[8,1,16,320]{3,0,2,1:T(8,128)(2,1)S(1)} collective-permute-done((bf16[8,1,16,320]{3,0,2,1:T(8,128)(2,1)S(1)}, bf16[8,1,16,320]{3,0,2,1:T(8,128)(2,1)S(1)}, u32[]{:S(2)}, u32[]{:S(2)}) %collective-permute-start.1) | collective-permute-done | bytes 81952 | tf_op jit(solution)/shard_map/ppermute | solution.py:15
  11.8 3.5 %multiply_convert_fusion.1 = bf16[8,8,16,320]{3,0,2,1:T(8,128)(2,1)S(1)} fusion(bf16[3,3,320,320]{3,2,1,0:T(8,128)(2,1)S(1)} %copy-done.13, bf16[8,1,16,320]{3,0,2,1:T(8,128)(2,1)S(1)} %collective-permute-done.1, bf16[8,8,16,320]{3,0,2,1:T(8,128)(2,1)S(1)} %add_convert_fusion, bf16[8,1,16,320]{3,0,2,1:T(8,128)(2,1)S(1)} %collective-permute-done, ...), kind=kOutput, calls=%fused_computation.14 | convolution fusion | flops 1813217280 | bytes 3319040 | tf_op jit(solution)/shard_map/conv_general_dilated | solution.py:28
  15.3 1.5 collective-permute-start.2
  16.8 1.3 collective-permute-start.3
  18.1 0.3 collective-permute-done.2
  18.5 3.7 %collective-permute-done.3 = bf16[8,1,16,320]{3,0,2,1:T(8,128)(2,1)S(1)} collective-permute-done((bf16[8,1,16,320]{3,0,2,1:T(8,128)(2,1)S(1)}, bf16[8,1,16,320]{3,0,2,1:T(8,128)(2,1)S(1)}, u32[]{:S(2)}, u32[]{:S(2)}) %collective-permute-start.3) | collective-permute-done | bytes 81952 | tf_op jit(solution)/shard_map/ppermute | solution.py:15
  22.2 4.5 %fusion.39 = (f32[8,8,16]{0,2,1:T(8,128)S(1)}, f32[8,8,16,320]{3,0,2,1:T(8,128)}) fusion(bf16[3,3,320,320]{3,2,1,0:T(8,128)(2,1)S(1)} %copy-done, bf16[8,1,16,320]{3,0,2,1:T(8,128)(2,1)S(1)} %collective-permute-done.3, bf16[8,8,16,320]{3,0,2,1:T(8,128)(2,1)S(1)} %multiply_convert_fusion.1, bf16[8,1,16,320]{3,0,2,1:T(8,128)(2,1)S(1)} %collective-permute-done.2, ...), kind=kOutput, calls=%fused_computation.86 | convolution fusion | flops 1812233216 | bytes 4632576 | tf_op jit(solution)/shard_map/conv_general_dilated | solution.py:28
  26.8 0.1 copy.50
  26.9 0.1 div.22
  27.0 1.8 copy.48
  28.9 0.4 multiply_reduce_fusion
  29.5 0.3 multiply_convert_fusion
  29.8 0.6 fusion.8
  30.4 0.1 copy.61
  30.5 0.9 copy-done.4
  31.4 0.9 copy_dynamic-update-slice_fusion.3
  32.3 0.6 fusion.9
  32.9 0.1 copy.62
  33.0 0.8 copy-done.6
  33.9 0.9 copy_dynamic-update-slice_fusion.1
  34.8 1.2 collective-permute-start.4
  36.0 4.7 %collective-permute-start.5 = (bf16[2,8,128,320]{2,3,1,0:T(8,128)(2,1)}, bf16[2,8,128,320]{2,3,1,0:T(8,128)(2,1)}, u32[]{:S(2)}, u32[]{:S(2)}) collective-permute-start(bf16[2,8,128,320]{2,3,1,0:T(8,128)(2,1)} %copy_dynamic-update-slice_fusion.1), channel_id=1, source_target_pairs={{30,0},{0,2},{2,4},{4,6},{6,8},{8,10},{10,12},{12,14},{14,16},{16,... | collective-permute-start | bytes 3932168 | tf_op jit(solution)/shard_map/ppermute | solution.py:23
  40.9 0.4 convolution_bitcast_fusion
  41.5 3.1 %collective-permute-start.7 = (bf16[2,8,128,320]{2,3,1,0:T(8,128)(2,1)}, bf16[2,8,128,320]{2,3,1,0:T(8,128)(2,1)}, u32[]{:S(2)}, u32[]{:S(2)}) collective-permute-start(bf16[2,8,128,320]{2,3,1,0:T(8,128)(2,1)} %copy_dynamic-update-slice_fusion.1), channel_id=1, source_target_pairs={{4,0},{6,2},{8,4},{10,6},{12,8},{14,10},{16,12},{18,14},{20,16},{2... | collective-permute-start | bytes 3932168 | tf_op jit(solution)/shard_map/ppermute | solution.py:23
  44.6 0.6 fusion.10
  45.2 0.1 copy.63
  45.3 4.2 %copy.54 = bf16[8,128,8,40]{3,0,2,1:T(8,128)(2,1)} copy(bf16[8,128,8,40]{1,0,3,2:T(8,128)(2,1)S(1)} %bitcast.63) | data formatting | bytes 1310720 | tf_op jit(solution)/shard_map/reshape;reshape | solution.py:44
  49.5 0.4 copy.59
  50.0 53.3 %collective-permute-done.4 = bf16[2,8,128,320]{2,3,1,0:T(8,128)(2,1)} collective-permute-done((bf16[2,8,128,320]{2,3,1,0:T(8,128)(2,1)}, bf16[2,8,128,320]{2,3,1,0:T(8,128)(2,1)}, u32[]{:S(2)}, u32[]{:S(2)}) %collective-permute-start.4) | collective-permute-done | bytes 1310752 | tf_op jit(solution)/shard_map/ppermute | solution.py:23
  103.3 1.4 constant_dynamic-update-slice_fusion.3
  104.7 16.4 %collective-permute-done.5 = bf16[2,8,128,320]{2,3,1,0:T(8,128)(2,1)} collective-permute-done((bf16[2,8,128,320]{2,3,1,0:T(8,128)(2,1)}, bf16[2,8,128,320]{2,3,1,0:T(8,128)(2,1)}, u32[]{:S(2)}, u32[]{:S(2)}) %collective-permute-start.5) | collective-permute-done | bytes 1310752 | tf_op jit(solution)/shard_map/ppermute | solution.py:23
  121.1 1.5 constant_dynamic-update-slice_fusion.2
  122.6 0.1 copy_dynamic-update-slice_fusion.2
  122.8 0.1 copy_dynamic-update-slice_fusion
  122.9 1.5 constant_dynamic-update-slice_fusion.1
  124.5 1.5 constant_dynamic-update-slice_fusion
  126.0 3.1 %fusion.36 = (bf16[1,40,128,320]{2,3,1,0:T(8,128)(2,1)}, bf16[1,40,128,320]{2,3,1,0:T(8,128)(2,1)}) fusion(bf16[2,40,128,320]{2,3,1,0:T(8,128)(2,1)S(1)} %constant_dynamic-update-slice_fusion), kind=kLoop, calls=%fused_computation.83 | loop fusion | bytes 13107200 | tf_op jit(solution)/shard_map/slice | solution.py:124
  129.1 15.4 %copy.55 = bf16[40,128,8,40]{3,0,2,1:T(8,128)(2,1)} copy(bf16[40,128,8,40]{1,3,2,0:T(8,128)(2,1)} %bitcast.57) | data formatting | bytes 6553600 | tf_op jit(solution)/shard_map/reshape;squeeze | solution.py:45
  144.5 15.6 %copy.57 = bf16[40,128,8,40]{3,0,2,1:T(8,128)(2,1)} copy(bf16[40,128,8,40]{1,3,2,0:T(8,128)(2,1)} %bitcast.56) | data formatting | bytes 6553600 | tf_op jit(solution)/shard_map/reshape;squeeze | solution.py:46
  160.0 10.6 %fusion.40 = (f32[128,8,8]{2,1,0:T(8,128)}, f32[128,8,8,40]{3,2,1,0:T(8,128)}) fusion(f32[8,8,40]{2,1,0:T(8,128)S(1)} %copy.56, pred[8,40]{1,0:T(8,128)(4,1)S(1)} %abs_compare_fusion, bf16[8,128,8,40]{3,0,2,1:T(8,128)(2,1)S(1)} %copy-done.2, bf16[40,128,8,40]{3,0,2,1:T(8,128)(2,1)} %copy.55), kind=kOutput, calls=%fused_computation.87 | convolution fusion | flops 27852840 | bytes 5286208 | tf_op jit(solution)/shard_map/sub | solution.py:58
  170.6 8.2 %convert_bitcast_fusion = bf16[8,128,8,40]{3,0,2,1:T(8,128)(2,1)S(1)} fusion(bf16[40,128,8,40]{3,0,2,1:T(8,128)(2,1)} %copy.57, f32[128,8,8,40]{3,2,1,0:T(8,128)} %get-tuple-element.14, f32[128,8,8]{2,1,0:T(8,128)} %get-tuple-element.13), kind=kOutput, calls=%fused_computation.6 | convolution fusion | flops 27197440 | bytes 5275648 | tf_op jit(solution)/shard_map/phij,jphd->iphd/dot_general | solution.py:60
  178.8 3.0 %copy.58 = bf16[8,128,8,40]{1,0,3,2:T(8,128)(2,1)} copy(bf16[8,128,8,40]{3,0,2,1:T(8,128)(2,1)S(1)} %convert_bitcast_fusion) | data formatting | bytes 1310720 | tf_op jit(solution)/shard_map/convert_element_type | solution.py:61
  181.8 2.9 %convolution_add_fusion = f32[1024,320]{0,1:T(8,128)} fusion(f32[1024,320]{0,1:T(8,128)S(1)} %copy.59, bf16[320,320]{1,0:T(8,128)(2,1)} %param.23, bf16[40,8,8,128]{3,2,1,0:T(8,128)(2,1)} %bitcast.62), kind=kOutput, calls=%fused_computation.17 | convolution fusion | flops 210042880 | bytes 3481600 | tf_op jit(solution)/shard_map/dot_general | solution.py:126
  184.8 2.9 %copy.60 = f32[1024,320]{1,0:T(8,128)} copy(f32[1024,320]{0,1:T(8,128)} %convolution_add_fusion) | data formatting | bytes 2621440 | tf_op jit(solution)/shard_map/add | solution.py:129
  (51 shorter events, 0.8 us)
Async XLA Ops:
  0.0 22.2 %copy-start = (bf16[3,3,320,320]{3,2,1,0:T(8,128)(2,1)S(1)}, bf16[3,3,320,320]{3,2,1,0:T(8,128)(2,1)}, u32[]{:S(2)}) copy-start(bf16[3,3,320,320]{3,2,1,0:T(8,128)(2,1)} %param.16) | copy-start | bytes 5529604
  0.0 8.4 %copy-start.8 = (f32[1000,320]{0,1:T(8,128)S(1)}, f32[1000,320]{0,1:T(8,128)}, u32[]{:S(2)}) copy-start(f32[1000,320]{0,1:T(8,128)} %param.17) | copy-start | bytes 3840004
  0.0 11.8 %copy-start.13 = (bf16[3,3,320,320]{3,2,1,0:T(8,128)(2,1)S(1)}, bf16[3,3,320,320]{3,2,1,0:T(8,128)(2,1)}, u32[]{:S(2)}) copy-start(bf16[3,3,320,320]{3,2,1,0:T(8,128)(2,1)} %param.15) | copy-start | bytes 5529604
  2.4 6.7 %collective-permute-start = (bf16[8,1,16,320]{3,0,2,1:T(8,128)(2,1)S(1)}, bf16[8,1,16,320]{3,0,2,1:T(8,128)(2,1)S(1)}, u32[]{:S(2)}, u32[]{:S(2)}) collective-permute-start(bf16[8,1,16,320]{3,0,2,1:T(8,128)(2,1)S(1)} %get-tuple-element.9), channel_id=1, source_target_pairs={{0,1},{2,3},{4,5},{6,7},{8,9},{10,11},{12,13},{14,15},{16,17},{18,... | collective-permute-start | bytes 245768 | tf_op jit(solution)/shard_map/ppermute | solution.py:12
  6.4 5.4 %collective-permute-start.1 = (bf16[8,1,16,320]{3,0,2,1:T(8,128)(2,1)S(1)}, bf16[8,1,16,320]{3,0,2,1:T(8,128)(2,1)S(1)}, u32[]{:S(2)}, u32[]{:S(2)}) collective-permute-start(bf16[8,1,16,320]{3,0,2,1:T(8,128)(2,1)S(1)} %get-tuple-element.10), channel_id=1, source_target_pairs={{1,0},{3,2},{5,4},{7,6},{9,8},{11,10},{13,12},{15,14},{17,16},{19,... | collective-permute-start | bytes 245768 | tf_op jit(solution)/shard_map/ppermute | solution.py:15
  15.3 3.2 %collective-permute-start.2 = (bf16[8,1,16,320]{3,0,2,1:T(8,128)(2,1)S(1)}, bf16[8,1,16,320]{3,0,2,1:T(8,128)(2,1)S(1)}, u32[]{:S(2)}, u32[]{:S(2)}) collective-permute-start(bf16[8,1,16,320]{3,0,2,1:T(8,128)(2,1)S(1)} %get-tuple-element.7), channel_id=1, source_target_pairs={{0,1},{2,3},{4,5},{6,7},{8,9},{10,11},{12,13},{14,15},{16,17},{18,... | collective-permute-start | bytes 245768 | tf_op jit(solution)/shard_map/ppermute | solution.py:12
  16.8 5.4 %collective-permute-start.3 = (bf16[8,1,16,320]{3,0,2,1:T(8,128)(2,1)S(1)}, bf16[8,1,16,320]{3,0,2,1:T(8,128)(2,1)S(1)}, u32[]{:S(2)}, u32[]{:S(2)}) collective-permute-start(bf16[8,1,16,320]{3,0,2,1:T(8,128)(2,1)S(1)} %get-tuple-element.8), channel_id=1, source_target_pairs={{1,0},{3,2},{5,4},{7,6},{9,8},{11,10},{13,12},{15,14},{17,16},{19,... | collective-permute-start | bytes 245768 | tf_op jit(solution)/shard_map/ppermute | solution.py:15
  27.0 1.9 %copy-start.3 = (f32[8,8,16,320]{3,0,2,1:T(8,128)S(1)}, f32[8,8,16,320]{3,0,2,1:T(8,128)}, u32[]{:S(2)}) copy-start(f32[8,8,16,320]{3,0,2,1:T(8,128)} %get-tuple-element.12) | copy-start | bytes 3932164
  27.0 2.5 %copy-start.12 = (f32[320]{0:T(512)S(1)}, f32[320]{0:T(512)}, u32[]{:S(2)}) copy-start(f32[320]{0:T(512)} %param.19) | copy-start | bytes 3844
  28.9 0.9 copy-start.9
  29.8 2.5 %copy-start.10 = (bf16[320,320]{1,0:T(8,128)(2,1)S(1)}, bf16[320,320]{1,0:T(8,128)(2,1)}, u32[]{:S(2)}) copy-start(bf16[320,320]{1,0:T(8,128)(2,1)} %param.22) | copy-start | bytes 614404
  30.5 0.9 copy-start.4
  32.3 8.6 %copy-start.14 = (f32[8,33]{1,0:T(8,128)S(1)}, f32[8,33]{1,0:T(8,128)}, u32[]{:S(2)}) copy-start(f32[8,33]{1,0:T(8,128)} %param.24) | copy-start | bytes 3172
  32.3 9.1 %copy-start.15 = (s32[128]{0:T(128)S(1)}, s32[128]{0:T(128)}, u32[]{:S(2)}) copy-start(s32[128]{0:T(128)} %param.25) | copy-start | bytes 1540
  32.3 12.3 %copy-start.11 = (bf16[320,320]{1,0:T(8,128)(2,1)S(1)}, bf16[320,320]{1,0:T(8,128)(2,1)}, u32[]{:S(2)}) copy-start(bf16[320,320]{1,0:T(8,128)(2,1)} %param.20) | copy-start | bytes 614404
  33.0 0.8 copy-start.6
  34.8 68.5 %collective-permute-start.4 = (bf16[2,8,128,320]{2,3,1,0:T(8,128)(2,1)}, bf16[2,8,128,320]{2,3,1,0:T(8,128)(2,1)}, u32[]{:S(2)}, u32[]{:S(2)}) collective-permute-start(bf16[2,8,128,320]{2,3,1,0:T(8,128)(2,1)} %copy_dynamic-update-slice_fusion.1), channel_id=1, source_target_pairs={{28,0},{30,2},{0,4},{2,6},{4,8},{6,10},{8,12},{10,14},{12,16},{14,... | collective-permute-start | bytes 3932168 | tf_op jit(solution)/shard_map/ppermute | solution.py:23
  36.0 85.1 %collective-permute-start.5 = (bf16[2,8,128,320]{2,3,1,0:T(8,128)(2,1)}, bf16[2,8,128,320]{2,3,1,0:T(8,128)(2,1)}, u32[]{:S(2)}, u32[]{:S(2)}) collective-permute-start(bf16[2,8,128,320]{2,3,1,0:T(8,128)(2,1)} %copy_dynamic-update-slice_fusion.1), channel_id=1, source_target_pairs={{30,0},{0,2},{2,4},{4,6},{6,8},{8,10},{10,12},{12,14},{14,16},{16,... | collective-permute-start | bytes 3932168 | tf_op jit(solution)/shard_map/ppermute | solution.py:23
  40.9 82.0 %collective-permute-start.6 = (bf16[2,8,128,320]{2,3,1,0:T(8,128)(2,1)}, bf16[2,8,128,320]{2,3,1,0:T(8,128)(2,1)}, u32[]{:S(2)}, u32[]{:S(2)}) collective-permute-start(bf16[2,8,128,320]{2,3,1,0:T(8,128)(2,1)} %copy_dynamic-update-slice_fusion.1), channel_id=1, source_target_pairs={{2,0},{4,2},{6,4},{8,6},{10,8},{12,10},{14,12},{16,14},{18,16},{20... | collective-permute-start | bytes 3932168 | tf_op jit(solution)/shard_map/ppermute | solution.py:23
  41.5 83.0 %collective-permute-start.7 = (bf16[2,8,128,320]{2,3,1,0:T(8,128)(2,1)}, bf16[2,8,128,320]{2,3,1,0:T(8,128)(2,1)}, u32[]{:S(2)}, u32[]{:S(2)}) collective-permute-start(bf16[2,8,128,320]{2,3,1,0:T(8,128)(2,1)} %copy_dynamic-update-slice_fusion.1), channel_id=1, source_target_pairs={{4,0},{6,2},{8,4},{10,6},{12,8},{14,10},{16,12},{18,14},{20,16},{2... | collective-permute-start | bytes 3932168 | tf_op jit(solution)/shard_map/ppermute | solution.py:23
  50.0 72.7 %copy-start.5 = (bf16[40,8,8,128]{3,2,1,0:T(8,128)(2,1)S(1)}, bf16[40,8,8,128]{3,2,1,0:T(8,128)(2,1)}, u32[]{:S(2)}) copy-start(bf16[40,8,8,128]{3,2,1,0:T(8,128)(2,1)} %copy-done.4) | copy-start | bytes 1966084
  104.7 18.1 %copy-start.7 = (bf16[40,8,8,128]{3,2,1,0:T(8,128)(2,1)S(1)}, bf16[40,8,8,128]{3,2,1,0:T(8,128)(2,1)}, u32[]{:S(2)}) copy-start(bf16[40,8,8,128]{3,2,1,0:T(8,128)(2,1)} %copy-done.6) | copy-start | bytes 1966084
  144.5 15.6 %copy-start.2 = (bf16[8,128,8,40]{3,0,2,1:T(8,128)(2,1)S(1)}, bf16[8,128,8,40]{3,0,2,1:T(8,128)(2,1)}, u32[]{:S(2)}) copy-start(bf16[8,128,8,40]{3,0,2,1:T(8,128)(2,1)} %copy.54) | copy-start | bytes 1966084
  181.8 5.9 %copy-start.1 = (bf16[3,3,320,320]{3,2,1,0:T(8,128)(2,1)S(1)}, bf16[3,3,320,320]{3,2,1,0:T(8,128)(2,1)}, u32[]{:S(2)}) copy-start(bf16[3,3,320,320]{3,2,1,0:T(8,128)(2,1)} %param.16) | copy-start | bytes 5529604
where the time goes:
time: 189 us; the launch traced here: 188 us
  waiting for transfers between devices  76.5 us (40%)
  local copies, waits for them, and re-layouts  57.3 us (30%)
  matrix products  32.4 us (17%)
  starting transfers between devices  17.1 us (9%)
  other arithmetic  3.37 us (2%)
    ppermute x4, waiting for transfers between devices, passed_along(): return lax.ppermute(block, axis, route)  69.7 us
    another operation x1, local copies, waits for them, and re-layouts, attend(): v4 = value.reshape(fk, pix, heads, dh)  15.6 us
    another operation x1, local copies, waits for them, and re-layouts, attend(): k4 = key.reshape(fk, pix, heads, dh)  15.4 us
    sub x1, matrix products, attend(): expo = jnp.exp(scores - top)  10.6 us
    ppermute x4, starting transfers between devices, passed_along(): return lax.ppermute(block, axis, route)  8.95 us
    dot_general x1, matrix products, attend(): jnp.einsum('phij,jphd->iphd', weights, v4, preferred_element_type=jnp.flo...  8.17 us
    conv_general_dilated x2, matrix products, conv_pass(): lax.conv_general_dilated(rimmed, weight, (1, 1), ((0, 0), (1, 1)), dimens...  7.97 us
    unnamed x41, local copies, waits for them, and re-layouts  7.77 us
  transfers between devices with their start and end apart: 8, of which 5 were waited for; matrix products, arithmetic and copies ran while one was open for 6% of the time, Pallas kernels for 0%

commit v1 on v0

v1 whole, which is shorter than its diff:
```python
import functools

import jax
import jax.numpy as jnp
import numpy as np
from jax import lax
from jax.experimental import pallas as pl
from jax.experimental.pallas import tpu as pltpu
from jax.sharding import PartitionSpec as P

MESH = pl.DeviceIdType.MESH
LOG2E = 1.4426950408889634
GROUP = 4
BF16 = jnp.bfloat16
F32 = jnp.float32


def taps(flat, cols):
    n = flat.shape[0]
    col = lax.broadcasted_iota(jnp.int32, flat.shape, 0) % cols
    left = jnp.where(col == 0, 0.0, pltpu.roll(flat, 1, 0))
    right = jnp.where(col == cols - 1, 0.0, pltpu.roll(flat, n - 1, 0))
    return jnp.concatenate([left.astype(BF16), flat.astype(BF16), right.astype(BF16)], axis=-1)


def front_kernel(
    nb, step,
    x_ref, c_ref, w1_ref, w2_ref, embed_ref, gain_ref, perm_ref,
    bo_ref, normed_ref,
    mpad, top, bottom, wide1, wide2, nf, send_sem, recv_sem,
):
    count, rows, cols, chans = x_ref.shape
    me = lax.axis_index("band")
    up, down = (me + nb - 1) % nb, (me + 1) % nb
    barrier = pltpu.get_barrier_semaphore()
    for other in (up, down):
        pl.semaphore_signal(barrier, inc=1, device_id={"band": other}, device_id_type=MESH)
    mpad[:, 2 : 2 + rows] = (x_ref[...].astype(F32) + c_ref[...].astype(F32)).astype(BF16)
    pl.semaphore_wait(barrier, 2)
    to_down = pltpu.make_async_remote_copy(
        src_ref=mpad.at[:, pl.ds(rows, 2)], dst_ref=top, send_sem=send_sem.at[0],
        recv_sem=recv_sem.at[0], device_id={"band": down}, device_id_type=MESH,
    )
    to_up = pltpu.make_async_remote_copy(
        src_ref=mpad.at[:, pl.ds(2, 2)], dst_ref=bottom, send_sem=send_sem.at[1],
        recv_sem=recv_sem.at[1], device_id={"band": up}, device_id_type=MESH,
    )
    to_down.start()
    to_up.start()
    to_down.wait()
    to_up.wait()
    has_top = (me > 0).astype(F32)
    has_bottom = (me < nb - 1).astype(F32)
    mpad[:, 0:2] = (top[...].astype(F32) * has_top).astype(BF16)
    mpad[:, 2 + rows : 4 + rows] = (bottom[...].astype(F32) * has_bottom).astype(BF16)

    def frames_step(i, carry):
        at = pl.ds(i * step, step)
        flat = mpad[at].reshape(step * (rows + 4) * cols, chans).astype(F32)
        wide1[...] = taps(flat, cols).reshape(wide1.shape)
        acc = embed_ref[...]
        for a in range(3):
            acc = acc + jnp.dot(
                wide1[:, a : a + rows + 2].reshape(step * (rows + 2) * cols, 3 * chans),
                w1_ref[a], preferred_element_type=F32,
            )
        act = acc / (1.0 + jnp.exp(-acc))
        row = (lax.broadcasted_iota(jnp.int32, act.shape, 0) // cols) % (rows + 2)
        inside = jnp.where(row == 0, has_top, jnp.where(row == rows + 1, has_bottom, 1.0))
        act = act * inside
        wide2[...] = taps(act, cols).reshape(wide2.shape)
        out = mpad[at, 2 : 2 + rows].reshape(step * rows * cols, chans).astype(F32)
        conv = None
        for a in range(3):
            part = jnp.dot(
                wide2[:, a : a + rows].reshape(step * rows * cols, 3 * chans),
                w2_ref[a], preferred_element_type=F32,
            )
            conv = part if conv is None else conv + part
        out = out + conv
        bo_ref[at] = out.reshape(step, rows, cols, chans)
        centre = out - jnp.mean(out, axis=1, keepdims=True)
        scale = lax.rsqrt(jnp.mean(centre * centre, axis=1, keepdims=True) + 1e-05)
        nf[at] = (centre * scale * gain_ref[...]).astype(BF16).reshape(step, rows, cols, chans)
        return carry

    lax.fori_loop(0, count // step, frames_step, 0)
    for y in range(rows):
        block = nf[:, y].reshape(count * cols, chans)
        normed_ref[y * count * cols : (y + 1) * count * cols] = jnp.dot(
            perm_ref[...], block, preferred_element_type=F32
        ).astype(BF16)


def back_kernel(
    n, heads, scale,
    normed_ref, bo_ref, wq_ref, wkv_ref, wo_ref, bias_ref, head_ref, perm_ref,
    out_ref,
    win, qbuf, kbuf, vbuf, att, got,
    send_a, recv_a, send_b, recv_b, send_d, recv_d,
):
    count, rows, cols, chans = bo_ref.shape
    part = win.shape[1]
    me = lax.axis_index("frame")
    r = me % GROUP
    base = me - r
    after, before = (me + GROUP) % n, (me + n - GROUP) % n
    mates = [base + (r + d) % GROUP for d in range(1, GROUP)]
    barrier = pltpu.get_barrier_semaphore()
    for other in mates + [after, before]:
        pl.semaphore_signal(barrier, inc=1, device_id={"frame": other}, device_id_type=MESH)
    pl.semaphore_wait(barrier, GROUP + 1)

    def quarter(j):
        return pl.ds(pl.multiple_of(j * part, part), part)

    def to_mate(j):
        return pltpu.make_async_remote_copy(
            src_ref=normed_ref.at[quarter(j)], dst_ref=win.at[2 + r], send_sem=send_a.at[j],
            recv_sem=recv_a.at[r], device_id={"frame": base + j}, device_id_type=MESH,
        )

    def from_mate(j):
        return pltpu.make_async_remote_copy(
            src_ref=normed_ref.at[quarter(j)], dst_ref=win.at[2 + j], send_sem=send_a.at[j],
            recv_sem=recv_a.at[j], device_id={"frame": base + j}, device_id_type=MESH,
        )

    def along(j):
        return pltpu.make_async_remote_copy(
            src_ref=win.at[2 + j], dst_ref=win.at[(j + 6) % 8], send_sem=send_b.at[j],
            recv_sem=recv_b.at[j], device_id={"frame": (me + GROUP * (2 * (j // 2) - 1) + n) % n},
            device_id_type=MESH,
        )

    def back_to(j):
        return pltpu.make_async_remote_copy(
            src_ref=att.at[j], dst_ref=got.at[r], send_sem=send_d.at[j],
            recv_sem=recv_d.at[r], device_id={"frame": base + j}, device_id_type=MESH,
        )

    def back_from(j):
        return pltpu.make_async_remote_copy(
            src_ref=att.at[j], dst_ref=got.at[j], send_sem=send_d.at[j],
            recv_sem=recv_d.at[j], device_id={"frame": base + j}, device_id_type=MESH,
        )

    others = [(r + d) % GROUP for d in range(1, GROUP)]
    for j in others:
        to_mate(j).start()
    win[2 + r] = normed_ref[quarter(r)]
    along(r).start()
    for j in others:
        from_mate(j).wait_recv()
        along(j).start()

    def project(slot):
        kv = jnp.dot(win[slot], wkv_ref[...], preferred_element_type=F32).astype(BF16)
        kbuf[slot] = kv[:, :chans]
        vbuf[slot] = kv[:, chans:]

    for j in range(GROUP):
        project(2 + j)
        qbuf[j] = jnp.dot(win[2 + j], wq_ref[...], preferred_element_type=F32).astype(BF16)
    for j in range(GROUP):
        to = (j + 6) % 8
        pltpu.make_async_remote_copy(
            src_ref=win.at[2 + j], dst_ref=win.at[to], send_sem=send_b.at[j],
            recv_sem=recv_b.at[j], device_id={"frame": after}, device_id_type=MESH,
        ).wait_recv()
        project(to)

    def pair(i, carry):
        at = pl.ds(pl.multiple_of(i * 16, 16), 16)
        q = qbuf[:, at].reshape(GROUP * 16, chans)
        k = kbuf[:, at].reshape(128, chans)
        v = vbuf[:, at].reshape(128, chans)
        qx = jnp.concatenate([q * head_ref[h] for h in range(heads)], axis=0)
        s = lax.dot_general(qx, k, (((1,), (1,)), ((), ())), preferred_element_type=F32)
        s = s * scale + bias_ref[...]
        e = jnp.exp2(s - jnp.max(s, axis=1, keepdims=True))
        w = (e * (1.0 / jnp.sum(e, axis=1, keepdims=True))).astype(BF16)
        w = jnp.concatenate([w[h * 64 : (h + 1) * 64] for h in range(heads)], axis=1)
        vx = jnp.concatenate([v * head_ref[h] for h in range(heads)], axis=0)
        o = jnp.dot(w, vx, preferred_element_type=F32).astype(BF16)
        att[:, at] = o.reshape(GROUP, 16, chans)
        return carry

    lax.fori_loop(0, part // 16, pair, 0)
    for j in others:
        back_to(j).start()
    got[r] = att[r]
    for j in others:
        back_from(j).wait_recv()
    for y in range(rows):
        size = count * cols
        first = y * size
        block = got[first // part, first % part : first % part + size]
        block = jnp.dot(perm_ref[...], block, preferred_element_type=F32).astype(BF16)
        mixed = jnp.dot(block, wo_ref[...], preferred_element_type=F32)
        out_ref[:, y] = bo_ref[:, y] + mixed.reshape(count, cols, chans)
    for j in others:
        to_mate(j).wait_send()
        back_to(j).wait_send()
    for j in range(GROUP):
        along(j).wait_send()


def bias_table(rel_bias, reach_group, count):
    heads, width = rel_bias.shape
    span = (width - 1) // 2
    q = np.arange(GROUP * 2 * count)
    k = np.arange((GROUP + 4) * 2 * count)
    q_frame = q // (2 * count) * count + q % count
    k_frame = k // (2 * count) * count + k % count - 2 * count
    delta = k_frame[None, :] - q_frame[:, None]
    same = (q // count % 2)[:, None] == (k // count % 2)[None, :]
    delta_j = jnp.asarray(delta, jnp.int32)
    reach_rows = jnp.broadcast_to(
        reach_group.reshape(GROUP, 1, count), (GROUP, 2, count)
    ).reshape(-1, 1)
    allowed = jnp.logical_and(jnp.abs(delta_j) <= reach_rows, jnp.asarray(same))
    table = (delta_j[None] + span == jnp.arange(width, dtype=jnp.int32)[:, None, None]).astype(F32)
    bias = jnp.einsum("hs,sij->hij", rel_bias * LOG2E, table, precision=lax.Precision.HIGHEST)
    return jnp.where(allowed[None], bias, -jnp.inf).reshape(heads * q.size, k.size)


def shards(
    n, nb,
    frames, control, conv_first, conv_second, time_table, step_index, norm_gain,
    w_query, w_key, w_value, w_out, rel_bias, reach,
):
    count, rows, cols, chans = frames.shape
    heads = rel_bias.shape[0]
    pixels = rows * cols
    part = count * pixels // GROUP
    embed = lax.dynamic_slice_in_dim(time_table, step_index[0], 1, axis=0)
    perm = np.zeros((count * cols, count * cols), np.float32)
    for f in range(count):
        for x in range(cols):
            perm[x * count + f, f * cols + x] = 1.0
    to_pixels = jnp.asarray(perm, BF16)
    to_frames = jnp.asarray(perm.T, BF16)
    head_of = np.arange(chans) // (chans // heads)
    head_mask = jnp.asarray(
        (head_of[None, None, :] == np.arange(heads)[:, None, None]).astype(np.float32), BF16
    )
    vmem = pl.BlockSpec(memory_space=pltpu.VMEM)
    step = 4
    block_out, normed = pl.pallas_call(
        functools.partial(front_kernel, nb, step),
        out_shape=(
            jax.ShapeDtypeStruct((count, rows, cols, chans), F32),
            jax.ShapeDtypeStruct((count * pixels, chans), BF16),
        ),
        in_specs=[vmem] * 7,
        out_specs=(vmem, vmem),
        scratch_shapes=[
            pltpu.VMEM((count, rows + 4, cols, chans), BF16),
            pltpu.VMEM((count, 2, cols, chans), BF16),
            pltpu.VMEM((count, 2, cols, chans), BF16),
            pltpu.VMEM((step, rows + 4, cols, 3 * chans), BF16),
            pltpu.VMEM((step, rows + 2, cols, 3 * chans), BF16),
            pltpu.VMEM((count, rows, cols, chans), BF16),
            pltpu.SemaphoreType.DMA((2,)),
            pltpu.SemaphoreType.DMA((2,)),
        ],
        compiler_params=pltpu.CompilerParams(
            collective_id=0, has_side_effects=True, vmem_limit_bytes=48 * 2**20
        ),
    )(
        frames, control, conv_first.reshape(3, 3 * chans, chans),
        conv_second.reshape(3, 3 * chans, chans), embed, norm_gain.reshape(1, chans), to_pixels,
    )
    start = lax.axis_index("frame") // GROUP * (GROUP * count)
    bias = bias_table(rel_bias, lax.dynamic_slice_in_dim(reach, start, GROUP * count), count)
    dma = pltpu.SemaphoreType.DMA((GROUP,))
    window = GROUP + 4
    out = pl.pallas_call(
        functools.partial(back_kernel, n, heads, LOG2E * (chans // heads) ** (-0.5)),
        out_shape=jax.ShapeDtypeStruct((count, rows, cols, chans), F32),
        in_specs=[vmem] * 8,
        out_specs=vmem,
        scratch_shapes=[
            pltpu.VMEM((window, part, chans), BF16),
            pltpu.VMEM((GROUP, part, chans), BF16),
            pltpu.VMEM((window, part, chans), BF16),
            pltpu.VMEM((window, part, chans), BF16),
            pltpu.VMEM((GROUP, part, chans), BF16),
            pltpu.VMEM((GROUP, part, chans), BF16),
            dma, dma, dma, dma, dma, dma,
        ],
        compiler_params=pltpu.CompilerParams(
            collective_id=1, has_side_effects=True, vmem_limit_bytes=48 * 2**20
        ),
    )(
        normed, block_out, w_query, jnp.concatenate([w_key, w_value], axis=1), w_out, bias,
        head_mask, to_frames,
    )
    return out


def solution(mesh):
    split = P("frame", "band", None, None)
    return jax.shard_map(
        functools.partial(shards, mesh.shape["frame"], mesh.shape["band"]),
        mesh=mesh,
        in_specs=(split, split) + (P(),) * 11,
        out_specs=split,
        check_vma=False,
    )
```

time: 189 us -> 84.5 us (0.45)
  waiting for transfers between devices: 76.5 us -> 0 us
  Pallas kernels: 0 us -> 66.7 us
  local copies, waits for them, and re-layouts: 57.3 us -> 12.4 us
  matrix products: 32.4 us -> 1.28 us
  starting transfers between devices: 17.1 us -> 0 us
    ppermute x8 -> x0, waiting for transfers between devices: 76.5 us -> none  [the longest x4 69.7 us: passed_along(): return lax.ppermute(block, axis, route)]
    pallas_call x0 -> x2, Pallas kernels: none -> 66.7 us  [the longest x1 44.2 us: shards(): pl.pallas_call(functools.partial(back_kernel, n, heads, LOG2E * (chans //...]
    another operation x4 -> x0, local copies, waits for them, and re-layouts: 36.1 us -> none  [the longest x1 15.6 us: attend(): v4 = value.reshape(fk, pix, heads, dh)]
    ppermute x8 -> x0, starting transfers between devices: 17.1 us -> none  [the longest x4 8.95 us: passed_along(): return lax.ppermute(block, axis, route)]
    dot_general x7 -> x1, matrix products: 13.9 us -> 1.28 us  [bias_table(): jnp.einsum('hs,sij->hij', rel_bias * LOG2E, table, precision=lax.Precisio...]
    sub x1 -> x0, matrix products: 10.6 us -> none  [attend(): expo = jnp.exp(scores - top)]
    conv_general_dilated x2 -> x0, matrix products: 7.97 us -> none  [conv_pass(): lax.conv_general_dilated(rimmed, weight, (1, 1), ((0, 0), (1, 1)), dimens...]
    add x2 -> x0, local copies, waits for them, and re-layouts: 4.76 us -> none  [the longest x1 2.93 us: shards(): return (flat + mixed).reshape(count, rows, cols, chans)]
  transfers between devices with their start and end apart: 8 -> 0, of which waited for: 5 -> 0; matrix products, arithmetic and copies ran while one was open for 6% -> 0% of each run, Pallas kernels for 0% -> 0%
where the time goes in v1:
time: 84.5 us; the launch traced here: 84 us
  Pallas kernels  66.7 us (79%)
  local copies, waits for them, and re-layouts  12.4 us (15%)
  other arithmetic  2.63 us (3%)
  matrix products  1.28 us (2%)
  between operations  0.94 us (1%)
    pallas_call x1, Pallas kernels, shards(): pl.pallas_call(functools.partial(back_kernel, n, heads, LOG2E * (chans //...  44.2 us
    pallas_call x1, Pallas kernels, shards(): pl.pallas_call(functools.partial(front_kernel, nb, step), out_shape=(jax....  22.5 us
    unnamed x24, local copies, waits for them, and re-layouts  5.02 us
    broadcast_in_dim x2, local copies, waits for them, and re-layouts, bias_table(): jnp.broadcast_to(reach_group.reshape(GROUP, 1, count), (GROUP, 2, count))  2.57 us

profile of v1, /device:TPU:1, one launch (start us, length us, event | category | flops | bytes accessed | tf_op | source)
XLA Modules:
  0.0 84.0 jit_solution(12201738254740913834)
XLA Ops:
  0.0 0.0 copy-start
  0.0 0.0 copy-start.7
  0.0 0.0 copy-start.1
  0.8 1.5 %dynamic_slice.7 = s32[32]{0:T(128)} dynamic-slice(s32[128]{0:T(128)} %param.30, s32[]{:T(128)S(6)} %select_n.17), dynamic_slice_sizes={32} | dynamic-slice | bytes 260 | tf_op jit(solution)/shard_map/dynamic_slice | solution.py:276
  2.3 1.2 %reshape.21.gain_ref = f32[1,320]{1,0:T(1,128)} reshape(f32[320]{0:T(512)} %param.24) | data formatting | bytes 2560 | tf_op jit(solution)/shard_map/reshape | solution.py:273
  3.6 1.3 %broadcast_in_dim.22 = s32[4,8]{1,0:T(4,128)} reshape(s32[32]{0:T(128)} %dynamic_slice.7) | data formatting | bytes 256 | tf_op jit(solution)/shard_map/broadcast_in_dim | solution.py:219
  4.9 1.3 %broadcast_in_dim.23 = s32[4,2,8]{2,1,0:T(2,128)} broadcast(s32[4,8]{1,0:T(4,128)} %broadcast_in_dim.22), dimensions={0,2} | broadcast | bytes 384 | tf_op jit(solution)/shard_map/broadcast_in_dim | solution.py:219
  6.1 1.3 %le.10 = s32[64]{0:T(128)} reshape(s32[4,2,8]{2,1,0:T(2,128)} %broadcast_in_dim.23) | data formatting | bytes 512 | tf_op jit(solution)/shard_map/le | solution.py:222
  7.4 1.4 %compare_and_fusion = pred[64,128]{1,0:T(8,128)(4,1)} fusion(pred[64,128]{1,0:T(32,128)(4,1)} %constant.49.clone, s32[64,128]{1,0:T(8,128)} %constant.52, s32[64]{0:T(128)} %le.10), kind=kLoop, calls=%fused_computation.5 | loop fusion | flops 16384 | bytes 49408 | tf_op jit(solution)/shard_map/and | solution.py:222
  8.9 0.0 copy-done
  8.9 0.8 constant_dynamic-slice_fusion
  9.6 1.6 %copy.21.embed_ref = f32[1,320]{1,0:T(1,128)} copy(f32[1,320]{0,1:T(8,128)} %constant_dynamic-slice_fusion) | data formatting | bytes 2560
  11.2 0.0 copy-start.9
  11.2 0.0 copy-start.10
  11.2 1.3 %fusion.1 = f32[8,64,128]{2,0,1:T(8,128)S(1)} fusion(s32[64,128]{1,0:T(8,128)} %constant.53, pred[64,128]{1,0:T(8,128)(4,1)} %compare_and_fusion, f32[8,33]{1,0:T(8,128)} %param.29), kind=kOutput, calls=%fused_computation.2 | convolution fusion | flops 26288392 | bytes 304160 | tf_op jit(solution)/shard_map/hs,sij->hij/dot_general | solution.py:224
  12.5 0.1 copy.20
  12.6 1.2 %pad_maximum_fusion.wkv_ref = bf16[320,640]{1,0:T(8,128)(2,1)S(1)} fusion(bf16[320,320]{1,0:T(8,128)(2,1)} %param.27, bf16[320,320]{1,0:T(8,128)(2,1)} %param.26), kind=kLoop, calls=%fused_computation.4 | loop fusion | flops 819200 | bytes 819200 | tf_op jit(solution)/shard_map/concatenate | solution.py:297
  13.8 0.0 copy-done.7
  13.8 0.0 copy-done.1
  13.8 0.0 copy-done.9
  13.8 0.0 copy-done.10
  13.8 0.0 copy-start.2
  13.8 1.1 %copy-done.2 = bf16[8,8,16,320]{3,2,1,0:T(8,128)(2,1)S(1)} copy-done((bf16[8,8,16,320]{3,2,1,0:T(8,128)(2,1)S(1)}, bf16[8,8,16,320]{3,2,1,0:T(8,128)(2,1)}, u32[]{:S(2)}) %copy-start.2) | copy-done | bytes 655384
  14.9 0.0 copy-start.3
  14.9 1.1 %copy-done.3 = bf16[8,8,16,320]{3,2,1,0:T(8,128)(2,1)S(1)} copy-done((bf16[8,8,16,320]{3,2,1,0:T(8,128)(2,1)S(1)}, bf16[8,8,16,320]{3,2,1,0:T(8,128)(2,1)}, u32[]{:S(2)}) %copy-start.3) | copy-done | bytes 655384
  16.1 0.0 copy-start.4
  16.1 0.0 copy-start.5
  16.1 0.0 copy-start.6
  16.1 0.0 copy-start.8
  16.1 22.5 %shard_map.172 = (f32[8,8,16,320]{3,2,1,0:T(8,128)S(1)}, bf16[1024,320]{1,0:T(8,128)(2,1)S(1)}) custom-call(bf16[8,8,16,320]{3,2,1,0:T(8,128)(2,1)S(1)} %copy-done.2, bf16[8,8,16,320]{3,2,1,0:T(8,128)(2,1)S(1)} %copy-done.3, bf16[3,960,320]{2,1,0:T(8,128)(2,1)S(1)} %bitcast.10, bf16[3,960,320]{2,1,0:T(8,128)(2,1)} %bitcast.12, f32[1,320]{1,0:T(1,128)S(1)} %copy-done.9, ...), custom_call_target="tpu_custom_call" | custom-call | tf_op jit(solution)/shard_map/pallas_call | solution.py:250
  38.6 0.0 copy-done.4
  38.6 0.0 copy-done.5
  38.6 0.0 copy-done.6
  38.6 0.0 copy-done.8
  38.6 44.2 %shard_map.173 = f32[8,8,16,320]{3,2,1,0:T(8,128)S(1)} custom-call(bf16[1024,320]{1,0:T(8,128)(2,1)S(1)} %get-tuple-element.7.normed_ref, f32[8,8,16,320]{3,2,1,0:T(8,128)S(1)} %get-tuple-element.8.bo_ref, bf16[320,320]{1,0:T(8,128)(2,1)S(1)} %copy-done.4, bf16[320,640]{1,0:T(8,128)(2,1)S(1)} %pad_maximum_fusion.wkv_ref, bf16[320,320]{1,0:T(8,128)(2,1)S(1)} %copy-done.5, ...), custom_call_target="tpu_custom_call" | custom-call | tf_op jit(solution)/shard_map/pallas_call | solution.py:279
  82.9 1.1 %copy.25 = f32[8,8,16,320]{3,2,1,0:T(8,128)} copy(f32[8,8,16,320]{3,2,1,0:T(8,128)S(1)} %shard_map.173) | data formatting | bytes 2621440
Async XLA Ops:
  0.0 8.9 %copy-start = (f32[1000,320]{0,1:T(8,128)S(1)}, f32[1000,320]{0,1:T(8,128)}, u32[]{:S(2)}) copy-start(f32[1000,320]{0,1:T(8,128)} %param.22) | copy-start | bytes 3840004
  0.0 13.8 %copy-start.7 = (bf16[128,128]{1,0:T(8,128)(2,1)S(1)}, bf16[128,128]{1,0:T(8,128)(2,1)}, u32[]{:S(2)}) copy-start(bf16[128,128]{1,0:T(8,128)(2,1)} %constant.45.clone.perm_ref) | copy-start | bytes 98308
  0.0 13.8 %copy-start.1 = (bf16[3,3,320,320]{3,2,1,0:T(8,128)(2,1)S(1)}, bf16[3,3,320,320]{3,2,1,0:T(8,128)(2,1)}, u32[]{:S(2)}) copy-start(bf16[3,3,320,320]{3,2,1,0:T(8,128)(2,1)} %param.20) | copy-start | bytes 5529604
  11.2 2.6 %copy-start.9 = (f32[1,320]{1,0:T(1,128)S(1)}, f32[1,320]{1,0:T(1,128)}, u32[]{:S(2)}) copy-start(f32[1,320]{1,0:T(1,128)} %copy.21.embed_ref) | copy-start | bytes 3844
  11.2 2.6 %copy-start.10 = (f32[1,320]{1,0:T(1,128)S(1)}, f32[1,320]{1,0:T(1,128)}, u32[]{:S(2)}) copy-start(f32[1,320]{1,0:T(1,128)} %reshape.21.gain_ref) | copy-start | bytes 3844
  13.8 1.1 %copy-start.2 = (bf16[8,8,16,320]{3,2,1,0:T(8,128)(2,1)S(1)}, bf16[8,8,16,320]{3,2,1,0:T(8,128)(2,1)}, u32[]{:S(2)}) copy-start(bf16[8,8,16,320]{3,2,1,0:T(8,128)(2,1)} %x_ref.1) | copy-start | bytes 1966084
  14.9 1.1 %copy-start.3 = (bf16[8,8,16,320]{3,2,1,0:T(8,128)(2,1)S(1)}, bf16[8,8,16,320]{3,2,1,0:T(8,128)(2,1)}, u32[]{:S(2)}) copy-start(bf16[8,8,16,320]{3,2,1,0:T(8,128)(2,1)} %c_ref.1) | copy-start | bytes 1966084
  16.1 22.5 %copy-start.4 = (bf16[320,320]{1,0:T(8,128)(2,1)S(1)}, bf16[320,320]{1,0:T(8,128)(2,1)}, u32[]{:S(2)}) copy-start(bf16[320,320]{1,0:T(8,128)(2,1)} %wq_ref.1) | copy-start | bytes 614404
  16.1 22.5 %copy-start.5 = (bf16[320,320]{1,0:T(8,128)(2,1)S(1)}, bf16[320,320]{1,0:T(8,128)(2,1)}, u32[]{:S(2)}) copy-start(bf16[320,320]{1,0:T(8,128)(2,1)} %wo_ref.1) | copy-start | bytes 614404
  16.1 22.5 %copy-start.6 = (bf16[128,128]{1,0:T(8,128)(2,1)S(1)}, bf16[128,128]{1,0:T(8,128)(2,1)}, u32[]{:S(2)}) copy-start(bf16[128,128]{1,0:T(8,128)(2,1)} %constant.46.clone.perm_ref) | copy-start | bytes 98308
  16.1 22.5 %copy-start.8 = (bf16[8,1,320]{2,1,0:T(2,128)(2,1)S(1)}, bf16[8,1,320]{2,1,0:T(2,128)(2,1)}, u32[]{:S(2)}) copy-start(bf16[8,1,320]{2,1,0:T(2,128)(2,1)} %constant.47.clone.head_ref) | copy-start | bytes 15364

commit v2 on v0

v2 whole, which is shorter than its diff:
```python
import functools

import jax
import jax.numpy as jnp
from jax import lax
from jax.experimental import pallas as pl
from jax.experimental.pallas import tpu as pltpu
from jax.sharding import PartitionSpec as P

MESH = pl.DeviceIdType.MESH
LOG2E = 1.4426950408889634
GROUP = 4
BF16 = jnp.bfloat16
F32 = jnp.float32


def taps(flat, cols):
    n = flat.shape[0]
    col = lax.broadcasted_iota(jnp.int32, flat.shape, 0) % cols
    left = jnp.where(col == 0, 0.0, pltpu.roll(flat, 1, 0))
    right = jnp.where(col == cols - 1, 0.0, pltpu.roll(flat, n - 1, 0))
    return jnp.concatenate([left.astype(BF16), flat.astype(BF16), right.astype(BF16)], axis=-1)


def kernel(
    n, nb, heads, span,
    x_hbm, c_hbm, w1_hbm, w2_hbm, table_hbm, wq_hbm, wk_hbm, wv_hbm, wo_hbm,
    step_ref, rel_ref, gain_ref, reach_ref,
    out_ref,
    x_ref, c_ref, w1_ref, w2_ref, table_ref, wq_ref, wk_ref, wv_ref, wo_ref,
    merged, top, bottom, wide1, wide2, block_out, ready, win, att, got, bias, load_sem,
    send_h, recv_h, send_a, recv_a, send_b, recv_b, send_d, recv_d,
):
    count, rows, cols, chans = x_ref.shape
    chunks = rows // 2
    quart = cols // GROUP
    part = 2 * quart * count
    size = GROUP * part
    slots = GROUP + 4
    me, mb = lax.axis_index("frame"), lax.axis_index("band")
    up, down = (mb + nb - 1) % nb, (mb + 1) % nb
    r = me % GROUP
    base = me - r
    after, before = (me + GROUP) % n, (me + n - GROUP) % n
    others = [(r + d) % GROUP for d in range(1, GROUP)]

    barrier = pltpu.get_barrier_semaphore()
    for other in (up, down):
        pl.semaphore_signal(barrier, inc=1, device_id={"band": other}, device_id_type=MESH)
    for other in [base + j for j in others] + [after, before]:
        pl.semaphore_signal(barrier, inc=1, device_id={"frame": other}, device_id_type=MESH)
    pairs = [
        (x_hbm, x_ref), (c_hbm, c_ref), (w1_hbm, w1_ref), (table_hbm, table_ref), (w2_hbm, w2_ref),
        (wq_hbm, wq_ref), (wk_hbm, wk_ref), (wv_hbm, wv_ref), (wo_hbm, wo_ref),
    ]
    loads = [pltpu.make_async_copy(s, d, load_sem.at[i]) for i, (s, d) in enumerate(pairs)]
    for load in loads:
        load.start()

    def halo(src, dst, i, other):
        return pltpu.make_async_remote_copy(
            src_ref=src, dst_ref=dst, send_sem=send_h.at[i], recv_sem=recv_h.at[i],
            device_id={"band": other}, device_id_type=MESH,
        )

    def share(j):
        return pl.ds(pl.multiple_of(j * part, part), part)

    def to_mate(k, j, slot, sem):
        return pltpu.make_async_remote_copy(
            src_ref=ready.at[k, share(j)], dst_ref=win.at[k, 2 + slot], send_sem=send_a.at[k, j],
            recv_sem=recv_a.at[k, sem], device_id={"frame": base + j}, device_id_type=MESH,
        )

    def along(k, j):
        return pltpu.make_async_remote_copy(
            src_ref=win.at[k, 2 + j], dst_ref=win.at[k, (j + 6) % 8], send_sem=send_b.at[k, j],
            recv_sem=recv_b.at[k, j], device_id={"frame": (me + GROUP * (2 * (j // 2) - 1) + n) % n},
            device_id_type=MESH,
        )

    def back_to(k, j, place, sem):
        return pltpu.make_async_remote_copy(
            src_ref=att.at[k, j], dst_ref=got.at[k, place], send_sem=send_d.at[k, j],
            recv_sem=recv_d.at[k, sem], device_id={"frame": base + j}, device_id_type=MESH,
        )

    loads[0].wait()
    loads[1].wait()
    merged[...] = (x_ref[...].astype(F32) + c_ref[...].astype(F32)).astype(BF16)
    pl.semaphore_wait(barrier, GROUP + 3)
    to_down = halo(merged.at[:, pl.ds(rows - 2, 2)], top, 0, down)
    to_up = halo(merged.at[:, pl.ds(0, 2)], bottom, 1, up)
    to_down.start()
    to_up.start()

    def widen(at, block):
        flat = block.astype(F32).reshape(-1, chans)
        wide1[:, at : at + block.shape[1]] = taps(flat, cols).reshape(block.shape[:3] + (3 * chans,))

    for y in range(0, rows, 2):
        widen(2 + y, merged[:, y : y + 2])

    steps = table_ref.shape[1]
    picked = (lax.broadcasted_iota(jnp.int32, (8, steps), 1) == step_ref[0]).astype(F32)
    loads[3].wait()
    embed = lax.dot_general(
        picked, table_ref[...], (((1,), (1,)), ((), ())),
        precision=lax.Precision.HIGHEST, preferred_element_type=F32,
    )[0:1]
    to = lax.broadcasted_iota(jnp.int32, (size, size), 0)
    of = lax.broadcasted_iota(jnp.int32, (size, size), 1)

    def source(i):
        quarter, y = i // part, (i // (quart * count)) % 2
        return (i % count) * (2 * cols) + y * cols + quarter * quart + (i // count) % quart

    to_pixels = (source(to) == of).astype(F32).astype(BF16)
    to_frames = (source(of) == to).astype(F32).astype(BF16)
    has_top = (mb > 0).astype(F32)
    has_bottom = (mb < nb - 1).astype(F32)
    loads[2].wait()

    def first_conv(m):
        acc = embed
        for a in range(3):
            acc = acc + jnp.dot(
                wide1[:, 2 * m + a : 2 * m + a + 2].reshape(size, 3 * chans), w1_ref[a],
                preferred_element_type=F32,
            )
        act = acc / (1.0 + jnp.exp(-acc))
        row = (lax.broadcasted_iota(jnp.int32, act.shape, 0) // cols) % 2
        if m == 0:
            act = act * jnp.where(row == 0, has_top, 1.0)
        if m == chunks:
            act = act * jnp.where(row == 1, has_bottom, 1.0)
        wide2[:, 2 * m : 2 * m + 2] = taps(act, cols).reshape(count, 2, cols, 3 * chans)

    def second_conv(j, k):
        out = merged[:, 2 * j : 2 * j + 2].reshape(size, chans).astype(F32)
        conv = None
        for a in range(3):
            part_sum = jnp.dot(
                wide2[:, 2 * j + a : 2 * j + a + 2].reshape(size, 3 * chans), w2_ref[a],
                preferred_element_type=F32,
            )
            conv = part_sum if conv is None else conv + part_sum
        out = out + conv
        block_out[:, 2 * j : 2 * j + 2] = out.reshape(count, 2, cols, chans)
        centre = out - jnp.mean(out, axis=1, keepdims=True)
        scale = lax.rsqrt(jnp.mean(centre * centre, axis=1, keepdims=True) + 1e-05)
        normed = (centre * scale * gain_ref[...].reshape(1, chans)).astype(BF16)
        ready[k] = jnp.dot(to_pixels, normed, preferred_element_type=F32).astype(BF16)
        for i in others:
            to_mate(k, i, r, r).start()
        win[k, 2 + r] = ready[k, share(r)]
        along(k, r).start()

    def forward(k):
        for i in others:
            to_mate(k, i, i, i).wait_recv()
            along(k, i).start()

    order = list(range(1, chunks - 1)) + [0, chunks - 1]
    first_conv(1)
    for k, j in enumerate(order):
        if j == 0:
            to_down.wait()
            to_up.wait()
            widen(0, top[...].astype(F32) * has_top)
            widen(2 + rows, bottom[...].astype(F32) * has_bottom)
            first_conv(0)
        else:
            first_conv(j + 1)
        if k == 0:
            loads[4].wait()
        second_conv(j, k)
        if k > 0:
            forward(k - 1)

    q = lax.broadcasted_iota(jnp.int32, (GROUP * 2 * count, slots * 2 * count), 0)
    c = lax.broadcasted_iota(jnp.int32, (GROUP * 2 * count, slots * 2 * count), 1)
    q_frame = q // (2 * count) * count + q % count
    delta = c // (2 * count) * count + c % count - 2 * count - q_frame
    total = reach_ref.shape[0]
    lane = lax.broadcasted_iota(jnp.int32, (q.shape[0], total), 1)
    q_of = lax.broadcasted_iota(jnp.int32, (q.shape[0], total), 0)
    q_of = q_of // (2 * count) * count + q_of % count + base * count
    limit = jnp.sum(
        jnp.where(lane == q_of, reach_ref[...].reshape(1, total).astype(F32), 0.0),
        axis=1, keepdims=True,
    )
    same = (q // count) % 2 == (c // count) % 2
    allowed = jnp.logical_and(jnp.abs(delta).astype(F32) <= limit, same)
    tables = [jnp.zeros(q.shape, F32) for _ in range(heads)]
    for s in range(2 * span + 1):
        hit = delta == s - span
        for h in range(heads):
            tables[h] = jnp.where(hit, rel_ref[h, s], tables[h])
    for h in range(heads):
        bias[h * q.shape[0] : (h + 1) * q.shape[0]] = jnp.where(
            allowed, tables[h] * LOG2E, -jnp.inf
        )
    forward(chunks - 1)

    for load in loads[5:]:
        load.wait()
    head_of = lax.broadcasted_iota(jnp.int32, (1, chans), 1) // (chans // heads)
    masks = [(head_of == h).astype(F32).astype(BF16) for h in range(heads)]
    scale = LOG2E * (chans // heads) ** (-0.5)
    edge = GROUP * 2 * count

    def attend(k, carry):
        for j in range(GROUP):
            along(k, j).wait_recv()
        field = win[k].reshape(slots * part, chans)
        keys = jnp.dot(field, wk_ref[...], preferred_element_type=F32)
        values = jnp.dot(field, wv_ref[...], preferred_element_type=F32)
        queries = jnp.dot(
            field[2 * part : (2 + GROUP) * part], wq_ref[...], preferred_element_type=F32
        )
        keys = keys.astype(BF16).reshape(slots, part, chans)
        values = values.astype(BF16).reshape(slots, part, chans)
        queries = queries.astype(BF16).reshape(GROUP, part, chans)
        for first in range(0, part, 2 * count):
            last = first + 2 * count
            qs = queries[:, first:last].reshape(edge, chans)
            ks = keys[:, first:last].reshape(slots * 2 * count, chans)
            vs = values[:, first:last].reshape(slots * 2 * count, chans)
            qx = jnp.concatenate([qs * mask for mask in masks], axis=0)
            s = lax.dot_general(qx, ks, (((1,), (1,)), ((), ())), preferred_element_type=F32)
            s = s * scale + bias[...]
            e = jnp.exp2(s - jnp.max(s, axis=1, keepdims=True))
            w = (e * (1.0 / jnp.sum(e, axis=1, keepdims=True))).astype(BF16)
            w = jnp.concatenate([w[h * edge : (h + 1) * edge] for h in range(heads)], axis=1)
            vx = jnp.concatenate([vs * mask for mask in masks], axis=0)
            o = jnp.dot(w, vx, preferred_element_type=F32).astype(BF16)
            att[k, :, first:last] = o.reshape(GROUP, 2 * count, chans)
        for j in others:
            back_to(k, j, r, r).start()
        got[k, r] = att[k, r]
        return carry

    lax.fori_loop(0, chunks, attend, 0)
    for k, y in enumerate(order):
        for j in others:
            back_to(k, j, j, j).wait_recv()
        block = got[k].reshape(size, chans)
        block = jnp.dot(to_frames, block, preferred_element_type=F32).astype(BF16)
        mixed = jnp.dot(block, wo_ref[...], preferred_element_type=F32)
        out_ref[:, 2 * y : 2 * y + 2] = block_out[:, 2 * y : 2 * y + 2] + mixed.reshape(
            count, 2, cols, chans
        )
    for k in range(chunks):
        for j in others:
            to_mate(k, j, r, r).wait_send()
            back_to(k, j, r, r).wait_send()
        for j in range(GROUP):
            along(k, j).wait_send()


def shards(
    n, nb,
    frames, control, conv_first, conv_second, time_table, step_index, norm_gain,
    w_query, w_key, w_value, w_out, rel_bias, reach,
):
    count, rows, cols, chans = frames.shape
    heads, width = rel_bias.shape
    chunks, part, slots = rows // 2, 2 * cols // GROUP * count, GROUP + 4
    table = time_table.T
    hbm = pl.BlockSpec(memory_space=pltpu.HBM)
    smem = pl.BlockSpec(memory_space=pltpu.SMEM)
    vmem = pl.BlockSpec(memory_space=pltpu.VMEM)
    wide = (3, 3 * chans, chans)
    square = pltpu.VMEM((chans, chans), BF16)
    dma = pltpu.SemaphoreType.DMA((chunks, GROUP))
    return pl.pallas_call(
        functools.partial(kernel, n, nb, heads, (width - 1) // 2),
        out_shape=jax.ShapeDtypeStruct((count, rows, cols, chans), F32),
        in_specs=[hbm] * 9 + [smem, smem, vmem, vmem],
        out_specs=vmem,
        scratch_shapes=[
            pltpu.VMEM(frames.shape, BF16),
            pltpu.VMEM(frames.shape, BF16),
            pltpu.VMEM(wide, BF16),
            pltpu.VMEM(wide, BF16),
            pltpu.VMEM(table.shape, F32),
            square, square, square, square,
            pltpu.VMEM(frames.shape, BF16),
            pltpu.VMEM((count, 2, cols, chans), BF16),
            pltpu.VMEM((count, 2, cols, chans), BF16),
            pltpu.VMEM((count, rows + 4, cols, 3 * chans), BF16),
            pltpu.VMEM((count, rows + 2, cols, 3 * chans), BF16),
            pltpu.VMEM(frames.shape, F32),
            pltpu.VMEM((chunks, GROUP * part, chans), BF16),
            pltpu.VMEM((chunks, slots, part, chans), BF16),
            pltpu.VMEM((chunks, GROUP, part, chans), BF16),
            pltpu.VMEM((chunks, GROUP, part, chans), BF16),
            pltpu.VMEM((heads * GROUP * 2 * count, slots * 2 * count), F32),
            pltpu.SemaphoreType.DMA((9,)),
            pltpu.SemaphoreType.DMA((2,)),
            pltpu.SemaphoreType.DMA((2,)),
            dma, dma, dma, dma, dma, dma,
        ],
        compiler_params=pltpu.CompilerParams(
            collective_id=0, has_side_effects=True, vmem_limit_bytes=56 * 2**20
        ),
    )(
        frames, control, conv_first.reshape(wide), conv_second.reshape(wide), table,
        w_query, w_key, w_value, w_out, step_index, rel_bias, norm_gain, reach,
    )


def solution(mesh):
    split = P("frame", "band", None, None)
    return jax.shard_map(
        functools.partial(shards, mesh.shape["frame"], mesh.shape["band"]),
        mesh=mesh,
        in_specs=(split, split) + (P(),) * 11,
        out_specs=split,
        check_vma=False,
    )
```

time: 189 us -> 46.8 us (0.25)
  waiting for transfers between devices: 76.5 us -> 0 us
  local copies, waits for them, and re-layouts: 57.3 us -> 2.67 us
  Pallas kernels: 0 us -> 43.3 us
  matrix products: 32.4 us -> 0 us
  starting transfers between devices: 17.1 us -> 0 us
  other arithmetic: 3.37 us -> 0 us
    ppermute x8 -> x0, waiting for transfers between devices: 76.5 us -> none  [the longest x4 69.7 us: passed_along(): return lax.ppermute(block, axis, route)]
    pallas_call x0 -> x1, Pallas kernels: none -> 43.3 us  [shards(): pl.pallas_call(functools.partial(kernel, n, nb, heads, (width - 1) // 2),...]
    another operation x4 -> x0, local copies, waits for them, and re-layouts: 36.1 us -> none  [the longest x1 15.6 us: attend(): v4 = value.reshape(fk, pix, heads, dh)]
    ppermute x8 -> x0, starting transfers between devices: 17.1 us -> none  [the longest x4 8.95 us: passed_along(): return lax.ppermute(block, axis, route)]
    dot_general x7 -> x0, matrix products: 13.9 us -> none  [the longest x1 8.17 us: attend(): jnp.einsum('phij,jphd->iphd', weights, v4, preferred_element_type=jnp.flo...]
    sub x1 -> x0, matrix products: 10.6 us -> none  [attend(): expo = jnp.exp(scores - top)]
    conv_general_dilated x2 -> x0, matrix products: 7.97 us -> none  [conv_pass(): lax.conv_general_dilated(rimmed, weight, (1, 1), ((0, 0), (1, 1)), dimens...]
    unnamed x41 -> x1, local copies, waits for them, and re-layouts: 7.77 us -> 2.67 us
  transfers between devices with their start and end apart: 8 -> 0, of which waited for: 5 -> 0; matrix products, arithmetic and copies ran while one was open for 6% -> 0% of each run, Pallas kernels for 0% -> 0%
where the time goes in v2:
time: 46.8 us; the launch traced here: 46.6 us
  Pallas kernels  43.3 us (93%)
  local copies, waits for them, and re-layouts  2.67 us (6%)
  between operations  0.66 us (1%)
    pallas_call x1, Pallas kernels, shards(): pl.pallas_call(functools.partial(kernel, n, nb, heads, (width - 1) // 2),...  43.3 us
    unnamed x1, local copies, waits for them, and re-layouts  2.67 us

profile of v2, /device:TPU:1, one launch (start us, length us, event | category | flops | bytes accessed | tf_op | source)
XLA Modules:
  0.0 46.6 jit_solution(12255140172882250494)
XLA Ops:
  0.7 43.3 %shard_map.127 = f32[8,8,16,320]{3,2,1,0:T(8,128)} custom-call(bf16[8,8,16,320]{3,2,1,0:T(8,128)(2,1)} %x_hbm.1, bf16[8,8,16,320]{3,2,1,0:T(8,128)(2,1)} %c_hbm.1, bf16[3,960,320]{2,1,0:T(8,128)(2,1)} %bitcast.3, bf16[3,960,320]{2,1,0:T(8,128)(2,1)} %bitcast.4, f32[320,1000]{1,0:T(8,128)} %bitcast.5, bf16[320,320]{1,0:T(8,128)(2,1)} %wq_hbm.1, ...), custom_call_target="tpu_custom_call" | custom-call | tf_op jit(solution)/shard_map/pallas_call | solution.py:277
  43.9 2.7 %copy.16 = f32[8,8,16,320]{3,2,1,0:T(8,128)} copy(f32[8,8,16,320]{3,2,1,0:T(8,128)} %shard_map.127) | data formatting | bytes 2621440

commit v3 on v2

--- a/solution.py
+++ b/solution.py
@@ -14,12 +14,16 @@
 F32 = jnp.float32
 
 
-def taps(flat, cols):
+def taps(block):
+    shape = block.shape
+    cols, chans = shape[2:]
+    flat = block.astype(F32).reshape(-1, chans)
     n = flat.shape[0]
-    col = lax.broadcasted_iota(jnp.int32, flat.shape, 0) % cols
-    left = jnp.where(col == 0, 0.0, pltpu.roll(flat, 1, 0))
-    right = jnp.where(col == cols - 1, 0.0, pltpu.roll(flat, n - 1, 0))
-    return jnp.concatenate([left.astype(BF16), flat.astype(BF16), right.astype(BF16)], axis=-1)
+    col = lax.broadcasted_iota(jnp.int32, (1, cols, chans), 1)
+    left = pltpu.roll(flat, 1, 0).reshape(-1, cols, chans) * (col > 0).astype(F32)
+    right = pltpu.roll(flat, n - 1, 0).reshape(-1, cols, chans) * (col < cols - 1).astype(F32)
+    sides = [left.astype(BF16), flat.astype(BF16).reshape(-1, cols, chans), right.astype(BF16)]
+    return jnp.concatenate(sides, axis=-1).reshape(shape[:3] + (3 * chans,))
 
 
 def kernel(
@@ -54,8 +58,8 @@
         (wq_hbm, wq_ref), (wk_hbm, wk_ref), (wv_hbm, wv_ref), (wo_hbm, wo_ref),
     ]
     loads = [pltpu.make_async_copy(s, d, load_sem.at[i]) for i, (s, d) in enumerate(pairs)]
-    for load in loads:
-        load.start()
+    loads[0].start()
+    loads[1].start()
 
     def halo(src, dst, i, other):
         return pltpu.make_async_remote_copy(
@@ -87,6 +91,8 @@
 
     loads[0].wait()
     loads[1].wait()
+    for load in loads[2:]:
+        load.start()
     merged[...] = (x_ref[...].astype(F32) + c_ref[...].astype(F32)).astype(BF16)
     pl.semaphore_wait(barrier, GROUP + 3)
     to_down = halo(merged.at[:, pl.ds(rows - 2, 2)], top, 0, down)
@@ -95,8 +101,7 @@
     to_up.start()
 
     def widen(at, block):
-        flat = block.astype(F32).reshape(-1, chans)
-        wide1[:, at : at + block.shape[1]] = taps(flat, cols).reshape(block.shape[:3] + (3 * chans,))
+        wide1[:, at : at + block.shape[1]] = taps(block)
 
     for y in range(0, rows, 2):
         widen(2 + y, merged[:, y : y + 2])
@@ -121,32 +126,46 @@
     has_bottom = (mb < nb - 1).astype(F32)
     loads[2].wait()
 
-    def first_conv(m):
-        acc = embed
+    def conv(wide, weight, spans):
+        out = None
         for a in range(3):
-            acc = acc + jnp.dot(
-                wide1[:, 2 * m + a : 2 * m + a + 2].reshape(size, 3 * chans), w1_ref[a],
-                preferred_element_type=F32,
-            )
+            rows_in = [
+                wide[:, at + a : at + a + extent].reshape(-1, 3 * chans) for at, extent in spans
+            ]
+            rows_in = rows_in[0] if len(spans) == 1 else jnp.concatenate(rows_in, axis=0)
+            term = jnp.dot(rows_in, weight[a], preferred_element_type=F32)
+            out = term if out is None else out + term
+        return out
+
+    def first_conv(spans):
+        acc = conv(wide1, w1_ref, spans) + embed
         act = acc / (1.0 + jnp.exp(-acc))
-        row = (lax.broadcasted_iota(jnp.int32, act.shape, 0) // cols) % 2
-        if m == 0:
-            act = act * jnp.where(row == 0, has_top, 1.0)
-        if m == chunks:
-            act = act * jnp.where(row == 1, has_bottom, 1.0)
-        wide2[:, 2 * m : 2 * m + 2] = taps(act, cols).reshape(count, 2, cols, 3 * chans)
-
-    def second_conv(j, k):
-        out = merged[:, 2 * j : 2 * j + 2].reshape(size, chans).astype(F32)
-        conv = None
-        for a in range(3):
-            part_sum = jnp.dot(
-                wide2[:, 2 * j + a : 2 * j + a + 2].reshape(size, 3 * chans), w2_ref[a],
-                preferred_element_type=F32,
-            )
-            conv = part_sum if conv is None else conv + part_sum
-        out = out + conv
-        block_out[:, 2 * j : 2 * j + 2] = out.reshape(count, 2, cols, chans)
+        begin = 0
+        for at, extent in spans:
+            block = act[begin : begin + count * extent * cols]
+            begin += count * extent * cols
+            block = block.reshape(count, extent, cols, chans)
+            row = lax.broadcasted_iota(jnp.int32, (1, extent, 1, chans), 1)
+            if at == 0:
+                block = block * jnp.where(row == 0, has_top, 1.0)
+            if at + extent == rows + 2:
+                block = block * jnp.where(row == extent - 1, has_bottom, 1.0)
+            wide2[:, at : at + extent] = taps(block)
+
+    def second_conv(spans, k):
+        sums = conv(wide2, w2_ref, spans)
+        begin = 0
+        for at, extent in spans:
+            block = sums[begin : begin + count * extent * cols]
+            begin += count * extent * cols
+            block = block.reshape(count, extent, cols, chans)
+            for y in range(0, extent, 2):
+                finish(block[:, y : y + 2].reshape(size, chans), at + y, k)
+                k += 1
+
+    def finish(summed, y, k):
+        out = merged[:, y : y + 2].reshape(size, chans).astype(F32) + summed
+        block_out[:, y : y + 2] = out.reshape(count, 2, cols, chans)
         centre = out - jnp.mean(out, axis=1, keepdims=True)
         scale = lax.rsqrt(jnp.mean(centre * centre, axis=1, keepdims=True) + 1e-05)
         normed = (centre * scale * gain_ref[...].reshape(1, chans)).astype(BF16)
@@ -162,21 +181,17 @@
             along(k, i).start()
 
     order = list(range(1, chunks - 1)) + [0, chunks - 1]
-    first_conv(1)
-    for k, j in enumerate(order):
-        if j == 0:
-            to_down.wait()
-            to_up.wait()
-            widen(0, top[...].astype(F32) * has_top)
-            widen(2 + rows, bottom[...].astype(F32) * has_bottom)
-            first_conv(0)
-        else:
-            first_conv(j + 1)
-        if k == 0:
-            loads[4].wait()
-        second_conv(j, k)
-        if k > 0:
-            forward(k - 1)
+    first_conv([(2, rows - 2)])
+    loads[4].wait()
+    second_conv([(2, rows - 4)], 0)
+    to_down.wait()
+    to_up.wait()
+    widen(0, top[...].astype(F32) * has_top)
+    widen(2 + rows, bottom[...].astype(F32) * has_bottom)
+    first_conv([(0, 2), (rows, 2)])
+    for k in range(chunks - 2):
+        forward(k)
+    second_conv([(0, 2), (rows - 2, 2)], chunks - 2)
 
     q = lax.broadcasted_iota(jnp.int32, (GROUP * 2 * count, slots * 2 * count), 0)
     c = lax.broadcasted_iota(jnp.int32, (GROUP * 2 * count, slots * 2 * count), 1)
@@ -201,6 +216,7 @@
         bias[h * q.shape[0] : (h + 1) * q.shape[0]] = jnp.where(
             allowed, tables[h] * LOG2E, -jnp.inf
         )
+    forward(chunks - 2)
     forward(chunks - 1)
 
     for load in loads[5:]:
@@ -209,6 +225,7 @@
     masks = [(head_of == h).astype(F32).astype(BF16) for h in range(heads)]
     scale = LOG2E * (chans // heads) ** (-0.5)
     edge = GROUP * 2 * count
+    ones = jnp.ones((slots * 2 * count, slots * 2 * count), BF16)
 
     def attend(k, carry):
         for j in range(GROUP):
@@ -231,7 +248,8 @@
             s = lax.dot_general(qx, ks, (((1,), (1,)), ((), ())), preferred_element_type=F32)
             s = s * scale + bias[...]
             e = jnp.exp2(s - jnp.max(s, axis=1, keepdims=True))
-            w = (e * (1.0 / jnp.sum(e, axis=1, keepdims=True))).astype(BF16)
+            e = e.astype(BF16)
+            w = (e.astype(F32) / jnp.dot(e, ones, preferred_element_type=F32)).astype(BF16)
             w = jnp.concatenate([w[h * edge : (h + 1) * edge] for h in range(heads)], axis=1)
             vx = jnp.concatenate([vs * mask for mask in masks], axis=0)
             o = jnp.dot(w, vx, preferred_element_type=F32).astype(BF16)

time: 46.8 us -> 49.5 us (1.058)
  Pallas kernels: 43.3 us -> 46 us
    pallas_call x1, Pallas kernels: 43.3 us -> 46 us  [shards(): pl.pallas_call(functools.partial(kernel, n, nb, heads, (width - 1) // 2),...]
where the time goes in v3:
time: 49.5 us; the launch traced here: 49.3 us
  Pallas kernels  46 us (93%)
  local copies, waits for them, and re-layouts  2.67 us (5%)
  between operations  0.66 us (1%)
    pallas_call x1, Pallas kernels, shards(): pl.pallas_call(functools.partial(kernel, n, nb, heads, (width - 1) // 2),...  46 us
    unnamed x1, local copies, waits for them, and re-layouts  2.67 us

profile of v3, /device:TPU:1, one launch (start us, length us, event | category | flops | bytes accessed | tf_op | source)
XLA Modules:
  0.0 49.3 jit_solution(12724023220379844067)
XLA Ops:
  0.7 46.0 %shard_map.127 = f32[8,8,16,320]{3,2,1,0:T(8,128)} custom-call(bf16[8,8,16,320]{3,2,1,0:T(8,128)(2,1)} %x_hbm.1, bf16[8,8,16,320]{3,2,1,0:T(8,128)(2,1)} %c_hbm.1, bf16[3,960,320]{2,1,0:T(8,128)(2,1)} %bitcast.3, bf16[3,960,320]{2,1,0:T(8,128)(2,1)} %bitcast.4, f32[320,1000]{1,0:T(8,128)} %bitcast.5, bf16[320,320]{1,0:T(8,128)(2,1)} %wq_hbm.1, ...), custom_call_target="tpu_custom_call" | custom-call | tf_op jit(solution)/shard_map/pallas_call | solution.py:295
  46.6 2.7 %copy.16 = f32[8,8,16,320]{3,2,1,0:T(8,128)} copy(f32[8,8,16,320]{3,2,1,0:T(8,128)} %shard_map.127) | data formatting | bytes 2621440

commit v4 on v2

--- a/solution.py
+++ b/solution.py
@@ -14,12 +14,16 @@
 F32 = jnp.float32
 
 
-def taps(flat, cols):
+def taps(block):
+    shape = block.shape
+    cols, chans = shape[2:]
+    flat = block.astype(F32).reshape(-1, chans)
     n = flat.shape[0]
-    col = lax.broadcasted_iota(jnp.int32, flat.shape, 0) % cols
-    left = jnp.where(col == 0, 0.0, pltpu.roll(flat, 1, 0))
-    right = jnp.where(col == cols - 1, 0.0, pltpu.roll(flat, n - 1, 0))
-    return jnp.concatenate([left.astype(BF16), flat.astype(BF16), right.astype(BF16)], axis=-1)
+    col = lax.broadcasted_iota(jnp.int32, (1, cols, chans), 1)
+    left = pltpu.roll(flat, 1, 0).reshape(-1, cols, chans) * (col > 0).astype(F32)
+    right = pltpu.roll(flat, n - 1, 0).reshape(-1, cols, chans) * (col < cols - 1).astype(F32)
+    sides = [left.astype(BF16), flat.astype(BF16).reshape(-1, cols, chans), right.astype(BF16)]
+    return jnp.concatenate(sides, axis=-1).reshape(shape[:3] + (3 * chans,))
 
 
 def kernel(
@@ -54,8 +58,8 @@
         (wq_hbm, wq_ref), (wk_hbm, wk_ref), (wv_hbm, wv_ref), (wo_hbm, wo_ref),
     ]
     loads = [pltpu.make_async_copy(s, d, load_sem.at[i]) for i, (s, d) in enumerate(pairs)]
-    for load in loads:
-        load.start()
+    loads[0].start()
+    loads[1].start()
 
     def halo(src, dst, i, other):
         return pltpu.make_async_remote_copy(
@@ -87,6 +91,8 @@
 
     loads[0].wait()
     loads[1].wait()
+    for load in loads[2:]:
+        load.start()
     merged[...] = (x_ref[...].astype(F32) + c_ref[...].astype(F32)).astype(BF16)
     pl.semaphore_wait(barrier, GROUP + 3)
     to_down = halo(merged.at[:, pl.ds(rows - 2, 2)], top, 0, down)
@@ -95,8 +101,7 @@
     to_up.start()
 
     def widen(at, block):
-        flat = block.astype(F32).reshape(-1, chans)
-        wide1[:, at : at + block.shape[1]] = taps(flat, cols).reshape(block.shape[:3] + (3 * chans,))
+        wide1[:, at : at + block.shape[1]] = taps(block)
 
     for y in range(0, rows, 2):
         widen(2 + y, merged[:, y : y + 2])
@@ -129,12 +134,13 @@
                 preferred_element_type=F32,
             )
         act = acc / (1.0 + jnp.exp(-acc))
-        row = (lax.broadcasted_iota(jnp.int32, act.shape, 0) // cols) % 2
+        act = act.reshape(count, 2, cols, chans)
+        row = lax.broadcasted_iota(jnp.int32, (1, 2, 1, chans), 1)
         if m == 0:
             act = act * jnp.where(row == 0, has_top, 1.0)
         if m == chunks:
             act = act * jnp.where(row == 1, has_bottom, 1.0)
-        wide2[:, 2 * m : 2 * m + 2] = taps(act, cols).reshape(count, 2, cols, 3 * chans)
+        wide2[:, 2 * m : 2 * m + 2] = taps(act)
 
     def second_conv(j, k):
         out = merged[:, 2 * j : 2 * j + 2].reshape(size, chans).astype(F32)
@@ -178,64 +184,75 @@
         if k > 0:
             forward(k - 1)
 
-    q = lax.broadcasted_iota(jnp.int32, (GROUP * 2 * count, slots * 2 * count), 0)
-    c = lax.broadcasted_iota(jnp.int32, (GROUP * 2 * count, slots * 2 * count), 1)
-    q_frame = q // (2 * count) * count + q % count
-    delta = c // (2 * count) * count + c % count - 2 * count - q_frame
+    held, seen = GROUP * count, slots * count
+    q = lax.broadcasted_iota(jnp.int32, (held, 2 * seen), 0)
+    c = lax.broadcasted_iota(jnp.int32, (held, 2 * seen), 1)
+    delta = c % seen - 2 * count - q
     total = reach_ref.shape[0]
-    lane = lax.broadcasted_iota(jnp.int32, (q.shape[0], total), 1)
-    q_of = lax.broadcasted_iota(jnp.int32, (q.shape[0], total), 0)
-    q_of = q_of // (2 * count) * count + q_of % count + base * count
+    lane = lax.broadcasted_iota(jnp.int32, (held, total), 1)
+    q_of = lax.broadcasted_iota(jnp.int32, (held, total), 0) + base * count
     limit = jnp.sum(
         jnp.where(lane == q_of, reach_ref[...].reshape(1, total).astype(F32), 0.0),
         axis=1, keepdims=True,
     )
-    same = (q // count) % 2 == (c // count) % 2
-    allowed = jnp.logical_and(jnp.abs(delta).astype(F32) <= limit, same)
-    tables = [jnp.zeros(q.shape, F32) for _ in range(heads)]
+    allowed = jnp.abs(delta).astype(F32) <= limit
+    first_half = c < seen
+    tables = [jnp.zeros(q.shape, F32) for _ in range(heads // 2)]
     for s in range(2 * span + 1):
         hit = delta == s - span
-        for h in range(heads):
-            tables[h] = jnp.where(hit, rel_ref[h, s], tables[h])
-    for h in range(heads):
-        bias[h * q.shape[0] : (h + 1) * q.shape[0]] = jnp.where(
-            allowed, tables[h] * LOG2E, -jnp.inf
-        )
+        for g in range(heads // 2):
+            both = jnp.where(first_half, rel_ref[2 * g, s], rel_ref[2 * g + 1, s])
+            tables[g] = jnp.where(hit, both, tables[g])
+    for g in range(heads // 2):
+        bias[g * held : (g + 1) * held] = jnp.where(allowed, tables[g] * LOG2E, -jnp.inf)
     forward(chunks - 1)
 
     for load in loads[5:]:
         load.wait()
     head_of = lax.broadcasted_iota(jnp.int32, (1, chans), 1) // (chans // heads)
-    masks = [(head_of == h).astype(F32).astype(BF16) for h in range(heads)]
+    pair_masks = [(head_of // 2 == g).astype(F32) for g in range(heads // 2)]
+    pair_bf16 = [mask.astype(BF16) for mask in pair_masks]
+    halves = [(head_of % 2 == i).astype(F32).astype(BF16) for i in range(2)]
     scale = LOG2E * (chans // heads) ** (-0.5)
-    edge = GROUP * 2 * count
+    own = lax.broadcasted_iota(jnp.int32, (2 * seen, 2 * seen), 0) // seen
+    own = own == lax.broadcasted_iota(jnp.int32, (2 * seen, 2 * seen), 1) // seen
+    ones = own.astype(F32).astype(BF16)
+    left = lax.broadcasted_iota(jnp.int32, (heads // 2 * held, 2 * seen), 1) < seen
 
     def attend(k, carry):
         for j in range(GROUP):
             along(k, j).wait_recv()
         field = win[k].reshape(slots * part, chans)
+        pixels = part // count
         keys = jnp.dot(field, wk_ref[...], preferred_element_type=F32)
         values = jnp.dot(field, wv_ref[...], preferred_element_type=F32)
         queries = jnp.dot(
             field[2 * part : (2 + GROUP) * part], wq_ref[...], preferred_element_type=F32
         )
-        keys = keys.astype(BF16).reshape(slots, part, chans)
-        values = values.astype(BF16).reshape(slots, part, chans)
-        queries = queries.astype(BF16).reshape(GROUP, part, chans)
-        for first in range(0, part, 2 * count):
-            last = first + 2 * count
-            qs = queries[:, first:last].reshape(edge, chans)
-            ks = keys[:, first:last].reshape(slots * 2 * count, chans)
-            vs = values[:, first:last].reshape(slots * 2 * count, chans)
-            qx = jnp.concatenate([qs * mask for mask in masks], axis=0)
-            s = lax.dot_general(qx, ks, (((1,), (1,)), ((), ())), preferred_element_type=F32)
+        keys = keys.reshape(slots, pixels, count, chans)
+        values = values.reshape(slots, pixels, count, chans)
+        queries = queries.reshape(GROUP, pixels, count, chans)
+        done = []
+        for p in range(pixels):
+            qs = queries[:, p].reshape(held, chans).astype(BF16)
+            ks = keys[:, p].reshape(seen, chans).astype(BF16)
+            vs = values[:, p].reshape(seen, chans).astype(BF16)
+            qx = jnp.concatenate([qs * mask for mask in pair_bf16], axis=0)
+            kx = jnp.concatenate([ks * mask for mask in halves], axis=0)
+            vx = jnp.concatenate([vs * mask for mask in halves], axis=0)
+            s = lax.dot_general(qx, kx, (((1,), (1,)), ((), ())), preferred_element_type=F32)
             s = s * scale + bias[...]
-            e = jnp.exp2(s - jnp.max(s, axis=1, keepdims=True))
-            w = (e * (1.0 / jnp.sum(e, axis=1, keepdims=True))).astype(BF16)
-            w = jnp.concatenate([w[h * edge : (h + 1) * edge] for h in range(heads)], axis=1)
-            vx = jnp.concatenate([vs * mask for mask in masks], axis=0)
-            o = jnp.dot(w, vx, preferred_element_type=F32).astype(BF16)
-            att[k, :, first:last] = o.reshape(GROUP, 2 * count, chans)
+            top_left = jnp.max(jnp.where(left, s, -jnp.inf), axis=1, keepdims=True)
+            top_right = jnp.max(jnp.where(left, -jnp.inf, s), axis=1, keepdims=True)
+            e = jnp.exp2(s - jnp.where(left, top_left, top_right)).astype(BF16)
+            w = (e.astype(F32) / jnp.dot(e, ones, preferred_element_type=F32)).astype(BF16)
+            o = jnp.dot(w, vx, preferred_element_type=F32)
+            o = sum(o[g * held : (g + 1) * held] * pair_masks[g] for g in range(heads // 2))
+            done.append(o.reshape(GROUP, count, chans))
+            if len(done) == 2:
+                first = (p - 1) * count
+                att[k, :, first : first + 2 * count] = jnp.concatenate(done, axis=1).astype(BF16)
+                done = []
         for j in others:
             back_to(k, j, r, r).start()
         got[k, r] = att[k, r]
@@ -296,7 +313,7 @@
             pltpu.VMEM((chunks, slots, part, chans), BF16),
             pltpu.VMEM((chunks, GROUP, part, chans), BF16),
             pltpu.VMEM((chunks, GROUP, part, chans), BF16),
-            pltpu.VMEM((heads * GROUP * 2 * count, slots * 2 * count), F32),
+            pltpu.VMEM((heads // 2 * GROUP * count, 2 * slots * count), F32),
             pltpu.SemaphoreType.DMA((9,)),
             pltpu.SemaphoreType.DMA((2,)),
             pltpu.SemaphoreType.DMA((2,)),

time: 46.8 us -> 50.2 us (1.073)
  Pallas kernels: 43.3 us -> 46.6 us
    pallas_call x1, Pallas kernels: 43.3 us -> 46.6 us  [shards(): pl.pallas_call(functools.partial(kernel, n, nb, heads, (width - 1) // 2),...]
where the time goes in v4:
time: 50.2 us; the launch traced here: 50 us
  Pallas kernels  46.6 us (93%)
  local copies, waits for them, and re-layouts  2.67 us (5%)
  between operations  0.66 us (1%)
    pallas_call x1, Pallas kernels, shards(): pl.pallas_call(functools.partial(kernel, n, nb, heads, (width - 1) // 2),...  46.6 us
    unnamed x1, local copies, waits for them, and re-layouts  2.67 us

profile of v4, /device:TPU:1, one launch (start us, length us, event | category | flops | bytes accessed | tf_op | source)
XLA Modules:
  0.0 50.0 jit_solution(16832693606889997656)
XLA Ops:
  0.7 46.6 %shard_map.127 = f32[8,8,16,320]{3,2,1,0:T(8,128)} custom-call(bf16[8,8,16,320]{3,2,1,0:T(8,128)(2,1)} %x_hbm.1, bf16[8,8,16,320]{3,2,1,0:T(8,128)(2,1)} %c_hbm.1, bf16[3,960,320]{2,1,0:T(8,128)(2,1)} %bitcast.3, bf16[3,960,320]{2,1,0:T(8,128)(2,1)} %bitcast.4, f32[320,1000]{1,0:T(8,128)} %bitcast.5, bf16[320,320]{1,0:T(8,128)(2,1)} %wq_hbm.1, ...), custom_call_target="tpu_custom_call" | custom-call | tf_op jit(solution)/shard_map/pallas_call | solution.py:294
  47.3 2.7 %copy.16 = f32[8,8,16,320]{3,2,1,0:T(8,128)} copy(f32[8,8,16,320]{3,2,1,0:T(8,128)} %shard_map.127) | data formatting | bytes 2621440

commit v5 on v4

--- a/solution.py
+++ b/solution.py
@@ -14,16 +14,12 @@
 F32 = jnp.float32
 
 
-def taps(block):
-    shape = block.shape
-    cols, chans = shape[2:]
-    flat = block.astype(F32).reshape(-1, chans)
+def taps(flat, cols):
     n = flat.shape[0]
-    col = lax.broadcasted_iota(jnp.int32, (1, cols, chans), 1)
-    left = pltpu.roll(flat, 1, 0).reshape(-1, cols, chans) * (col > 0).astype(F32)
-    right = pltpu.roll(flat, n - 1, 0).reshape(-1, cols, chans) * (col < cols - 1).astype(F32)
-    sides = [left.astype(BF16), flat.astype(BF16).reshape(-1, cols, chans), right.astype(BF16)]
-    return jnp.concatenate(sides, axis=-1).reshape(shape[:3] + (3 * chans,))
+    col = lax.broadcasted_iota(jnp.int32, flat.shape, 0) % cols
+    left = jnp.where(col == 0, 0.0, pltpu.roll(flat, 1, 0))
+    right = jnp.where(col == cols - 1, 0.0, pltpu.roll(flat, n - 1, 0))
+    return jnp.concatenate([left.astype(BF16), flat.astype(BF16), right.astype(BF16)], axis=-1)
 
 
 def kernel(
@@ -58,8 +54,8 @@
         (wq_hbm, wq_ref), (wk_hbm, wk_ref), (wv_hbm, wv_ref), (wo_hbm, wo_ref),
     ]
     loads = [pltpu.make_async_copy(s, d, load_sem.at[i]) for i, (s, d) in enumerate(pairs)]
-    loads[0].start()
-    loads[1].start()
+    for load in loads:
+        load.start()
 
     def halo(src, dst, i, other):
         return pltpu.make_async_remote_copy(
@@ -91,8 +87,6 @@
 
     loads[0].wait()
     loads[1].wait()
-    for load in loads[2:]:
-        load.start()
     merged[...] = (x_ref[...].astype(F32) + c_ref[...].astype(F32)).astype(BF16)
     pl.semaphore_wait(barrier, GROUP + 3)
     to_down = halo(merged.at[:, pl.ds(rows - 2, 2)], top, 0, down)
@@ -101,7 +95,8 @@
     to_up.start()
 
     def widen(at, block):
-        wide1[:, at : at + block.shape[1]] = taps(block)
+        flat = block.astype(F32).reshape(-1, chans)
+        wide1[:, at : at + block.shape[1]] = taps(flat, cols).reshape(block.shape[:3] + (3 * chans,))
 
     for y in range(0, rows, 2):
         widen(2 + y, merged[:, y : y + 2])
@@ -134,13 +129,12 @@
                 preferred_element_type=F32,
             )
         act = acc / (1.0 + jnp.exp(-acc))
-        act = act.reshape(count, 2, cols, chans)
-        row = lax.broadcasted_iota(jnp.int32, (1, 2, 1, chans), 1)
+        row = (lax.broadcasted_iota(jnp.int32, act.shape, 0) // cols) % 2
         if m == 0:
             act = act * jnp.where(row == 0, has_top, 1.0)
         if m == chunks:
             act = act * jnp.where(row == 1, has_bottom, 1.0)
-        wide2[:, 2 * m : 2 * m + 2] = taps(act)
+        wide2[:, 2 * m : 2 * m + 2] = taps(act, cols).reshape(count, 2, cols, 3 * chans)
 
     def second_conv(j, k):
         out = merged[:, 2 * j : 2 * j + 2].reshape(size, chans).astype(F32)
@@ -217,7 +211,7 @@
     own = lax.broadcasted_iota(jnp.int32, (2 * seen, 2 * seen), 0) // seen
     own = own == lax.broadcasted_iota(jnp.int32, (2 * seen, 2 * seen), 1) // seen
     ones = own.astype(F32).astype(BF16)
-    left = lax.broadcasted_iota(jnp.int32, (heads // 2 * held, 2 * seen), 1) < seen
+    left = lax.broadcasted_iota(jnp.int32, (part // count * (heads // 2) * held, 2 * seen), 1) < seen
 
     def attend(k, carry):
         for j in range(GROUP):
@@ -232,27 +226,39 @@
         keys = keys.reshape(slots, pixels, count, chans)
         values = values.reshape(slots, pixels, count, chans)
         queries = queries.reshape(GROUP, pixels, count, chans)
-        done = []
+        edge = heads // 2 * held
+        scores = []
         for p in range(pixels):
             qs = queries[:, p].reshape(held, chans).astype(BF16)
             ks = keys[:, p].reshape(seen, chans).astype(BF16)
-            vs = values[:, p].reshape(seen, chans).astype(BF16)
             qx = jnp.concatenate([qs * mask for mask in pair_bf16], axis=0)
             kx = jnp.concatenate([ks * mask for mask in halves], axis=0)
+            scores.append(
+                lax.dot_general(qx, kx, (((1,), (1,)), ((), ())), preferred_element_type=F32)
+                * scale + bias[...]
+            )
+        s = jnp.concatenate(scores, axis=0)
+        top_left = jnp.max(jnp.where(left, s, -jnp.inf), axis=1, keepdims=True)
+        top_right = jnp.max(jnp.where(left, -jnp.inf, s), axis=1, keepdims=True)
+        e = jnp.exp2(s - jnp.where(left, top_left, top_right)).astype(BF16)
+        w = (e.astype(F32) / jnp.dot(e, ones, preferred_element_type=F32)).astype(BF16)
+        mixed = []
+        for p in range(pixels):
+            vs = values[:, p].reshape(seen, chans).astype(BF16)
             vx = jnp.concatenate([vs * mask for mask in halves], axis=0)
-            s = lax.dot_general(qx, kx, (((1,), (1,)), ((), ())), preferred_element_type=F32)
-            s = s * scale + bias[...]
-            top_left = jnp.max(jnp.where(left, s, -jnp.inf), axis=1, keepdims=True)
-            top_right = jnp.max(jnp.where(left, -jnp.inf, s), axis=1, keepdims=True)
-            e = jnp.exp2(s - jnp.where(left, top_left, top_right)).astype(BF16)
-            w = (e.astype(F32) / jnp.dot(e, ones, preferred_element_type=F32)).astype(BF16)
-            o = jnp.dot(w, vx, preferred_element_type=F32)
-            o = sum(o[g * held : (g + 1) * held] * pair_masks[g] for g in range(heads // 2))
-            done.append(o.reshape(GROUP, count, chans))
-            if len(done) == 2:
-                first = (p - 1) * count
-                att[k, :, first : first + 2 * count] = jnp.concatenate(done, axis=1).astype(BF16)
-                done = []
+            mixed.append(
+                jnp.dot(w[p * edge : (p + 1) * edge], vx, preferred_element_type=F32)
+            )
+        mixed = [
+            sum(o[g * held : (g + 1) * held] * pair_masks[g] for g in range(heads // 2)).reshape(
+                GROUP, count, chans
+            )
+            for o in mixed
+        ]
+        for p in range(0, pixels, 2):
+            att[k, :, p * count : (p + 2) * count] = jnp.concatenate(
+                mixed[p : p + 2], axis=1
+            ).astype(BF16)
         for j in others:
             back_to(k, j, r, r).start()
         got[k, r] = att[k, r]

time: 50.2 us -> 43.8 us (0.87)
  Pallas kernels: 46.6 us -> 40.3 us
    pallas_call x1, Pallas kernels: 46.6 us -> 40.3 us  [shards(): pl.pallas_call(functools.partial(kernel, n, nb, heads, (width - 1) // 2),...]
where the time goes in v5:
time: 43.8 us; the launch traced here: 43.6 us
  Pallas kernels  40.3 us (92%)
  local copies, waits for them, and re-layouts  2.67 us (6%)
  between operations  0.66 us (2%)
    pallas_call x1, Pallas kernels, shards(): pl.pallas_call(functools.partial(kernel, n, nb, heads, (width - 1) // 2),...  40.3 us
    unnamed x1, local copies, waits for them, and re-layouts  2.67 us

profile of v5, /device:TPU:1, one launch (start us, length us, event | category | flops | bytes accessed | tf_op | source)
XLA Modules:
  0.0 43.6 jit_solution(4707627376964871677)
XLA Ops:
  0.7 40.3 %shard_map.127 = f32[8,8,16,320]{3,2,1,0:T(8,128)} custom-call(bf16[8,8,16,320]{3,2,1,0:T(8,128)(2,1)} %x_hbm.1, bf16[8,8,16,320]{3,2,1,0:T(8,128)(2,1)} %c_hbm.1, bf16[3,960,320]{2,1,0:T(8,128)(2,1)} %bitcast.3, bf16[3,960,320]{2,1,0:T(8,128)(2,1)} %bitcast.4, f32[320,1000]{1,0:T(8,128)} %bitcast.5, bf16[320,320]{1,0:T(8,128)(2,1)} %wq_hbm.1, ...), custom_call_target="tpu_custom_call" | custom-call | tf_op jit(solution)/shard_map/pallas_call | solution.py:300
  40.9 2.7 %copy.16 = f32[8,8,16,320]{3,2,1,0:T(8,128)} copy(f32[8,8,16,320]{3,2,1,0:T(8,128)} %shard_map.127) | data formatting | bytes 2621440
